TPU v7x, 256 devices: a whole 4x4x8 slice. The times are simulated.
256 devices in a mesh: fsdp: 32 (over z_hi, x, core), tp: 8 (over y, z_lo).
Axes of the slice: x: 4, y: 4, z: 8 (z_hi: 4, z_lo: 2; z = z_hi * 2 + z_lo), core: 2. Of those that a mesh axis runs over, the one named last changes fastest.
Arguments:
- activations: bfloat16 [8192, 8192], P('fsdp'), may hold values from -6 to 6
- grad_output: bfloat16 [8192, 28672], P('fsdp', 'tp'), may hold values from -0.1875 to 0.1875
- projector: bfloat16 [8192, 1024], P('fsdp'), may hold values from -0.125 to 0.125
- first_moment: float32 [1024, 28672], P('fsdp', 'tp'), may hold values from -0.625 to 0.625
- second_moment: float32 [1024, 28672], P('fsdp', 'tp'), may hold values from 0.01 to 0.5
Outputs:
- new_first: float32 [1024, 28672], P('fsdp', 'tp')
- new_second: float32 [1024, 28672], P('fsdp', 'tp')
- weight_update: bfloat16 [8192, 28672], P('fsdp', 'tp')
All inputs are finite; a program needn't handle non-finite values.
Results may differ from a plain program's by a relative error of at most 0.0059.
Values may be sent and summed in bfloat16 or wider, within the bound.
No kernel may reach another device: no remote copies, remote signals or barrier semaphores. Data moves between devices by JAX's collectives and lax.ppermute only.
A program may use at most 64 MiB of HBM per device.

v0:
```python
import functools

import jax
import jax.numpy as jnp
from jax import lax
from jax.experimental import pallas as pl
from jax.experimental.pallas import tpu as pltpu
from jax.sharding import PartitionSpec as P

first_fix = 0.9999734386011124
second_fix = 0.6339676587267705
BF = jnp.bfloat16
F32 = jnp.float32
MIB = 2**20


def swap(array, axis, mask):
    count = lax.axis_size(axis)
    return lax.ppermute(array, axis, [(i, i ^ mask) for i in range(count)])


def doubled(masks):
    order = [0]
    for mask in masks:
        order = order + [o ^ mask for o in order]
    return order


def table(order):
    return jnp.array(order, dtype=jnp.int32)


def by_core(core, own, other, axis):
    return jnp.where(
        core == 0,
        jnp.concatenate([own, other], axis=axis),
        jnp.concatenate([other, own], axis=axis),
    )


def call(kernel, outs, args, flops=0, vmem=16, scratch=(), smem=0, after=()):
    moved = sum(a.size * a.dtype.itemsize for a in args)
    moved += sum(o.size * o.dtype.itemsize for o in outs)
    specs = [
        pl.BlockSpec(memory_space=pltpu.SMEM if i < smem else pltpu.VMEM)
        for i in range(len(args))
    ]
    count = len(args)

    def body(*refs):
        kernel(*refs[:count], *refs[count + len(after) :])

    specs += [pl.BlockSpec(memory_space=pl.ANY) for _ in after]
    return pl.pallas_call(
        body,
        out_shape=list(outs),
        in_specs=specs,
        out_specs=[pl.BlockSpec(memory_space=pltpu.VMEM) for _ in outs],
        scratch_shapes=list(scratch),
        compiler_params=pltpu.CompilerParams(vmem_limit_bytes=vmem * MIB),
        cost_estimate=pl.CostEstimate(flops=flops, bytes_accessed=moved, transcendentals=0),
    )(*args, *after)


def shape(rows, columns, kind):
    return jax.ShapeDtypeStruct((rows, columns), kind)


def stack_kernel(sizes, *refs):
    outs = refs[sum(sizes) :]
    at = 0
    for size, out_ref in zip(sizes, outs):
        row = 0
        for ref in refs[at : at + size]:
            out_ref[row : row + ref.shape[0], :] = ref[...]
            row += ref.shape[0]
        at += size


def stack(groups):
    outs = [shape(sum(a.shape[0] for a in g), g[0].shape[1], g[0].dtype) for g in groups]
    return call(
        functools.partial(stack_kernel, [len(g) for g in groups]),
        outs,
        [a for g in groups for a in g],
    )


def reorder_kernel(width, index_ref, in_ref, out_ref):
    for k in range(out_ref.shape[1] // width):
        start = pl.multiple_of(index_ref[k] * width, width)
        out_ref[:, k * width : (k + 1) * width] = in_ref[:, pl.ds(start, width)]


def reorder(array, index, width):
    outs = [shape(array.shape[0], array.shape[1], array.dtype)]
    return call(
        functools.partial(reorder_kernel, width), outs, [index, array], vmem=24, smem=1
    )[0]


def sums_kernel(count, block, index_ref, own_ref, other_ref, grads_ref, *refs):
    outs, chosen = refs[:count], refs[count]
    tokens = own_ref.shape[1]
    at = 0
    for part, out_ref in enumerate(outs):
        blocks = out_ref.shape[0] // block
        for k in range(blocks):
            start = pl.multiple_of(index_ref[part * blocks + k] * block, block)
            chosen[k * block : (k + 1) * block, :tokens] = own_ref[pl.ds(start, block), :]
            chosen[k * block : (k + 1) * block, tokens:] = other_ref[pl.ds(start, block), :]
        width = out_ref.shape[1]
        out_ref[...] = jnp.dot(
            chosen[...], grads_ref[:, at : at + width], preferred_element_type=F32
        ).astype(out_ref.dtype)
        at += width


def partial_sums(index, own, other, grads, rows, widths, block, kind, after=()):
    return call(
        functools.partial(sums_kernel, len(widths), block),
        [shape(rows, w, kind) for w in widths],
        [index, own, other, grads],
        flops=2 * rows * grads.size,
        vmem=24,
        scratch=[pltpu.VMEM((rows, 2 * own.shape[1]), BF)],
        smem=1,
        after=after,
    )


def halve_kernel(count, *refs):
    kept, got, kept_out, sent = (refs[i * count : (i + 1) * count] for i in range(4))
    for k, g, o, s in zip(kept, got, kept_out, sent):
        rows = o.shape[0]
        s[...] = (k[rows:, :] + g[rows:, :].astype(F32)).astype(s.dtype)
        o[...] = k[:rows, :] + g[:rows, :].astype(F32)


def halve(kept, got):
    rows = kept[0].shape[0] // 2
    outs = [shape(rows, k.shape[1], kind) for kind in (F32, BF) for k in kept]
    result = call(functools.partial(halve_kernel, len(kept)), outs, list(kept) + list(got))
    return result[: len(kept)], result[len(kept) :]


def adam_kernel(count, *refs):
    kept, got = refs[:count], refs[count : 2 * count]
    first_ref, second_ref = refs[2 * count : 2 * count + 2]
    new_first_ref, new_second_ref = refs[2 * count + 2 : 2 * count + 4]
    directions = refs[2 * count + 4 :]
    at = 0
    for k, g, d in zip(kept, got, directions):
        span = slice(at, at + k.shape[1])
        at += k.shape[1]
        lowrank = k[...] + g[...].astype(F32)
        new_first = 0.9 * first_ref[:, span] + 0.1 * lowrank
        new_second = 0.99 * second_ref[:, span] + 0.01 * lowrank * lowrank
        new_first_ref[:, span] = new_first
        new_second_ref[:, span] = new_second
        d[...] = (new_first / first_fix / (jnp.sqrt(new_second / second_fix) + 1e-08)).astype(
            d.dtype
        )


def adam(kept, got, first, second):
    outs = [shape(*first.shape, F32)] * 2 + [shape(*k.shape, BF) for k in kept]
    result = call(
        functools.partial(adam_kernel, len(kept)), outs, [*kept, *got, first, second]
    )
    return result[0], result[1], result[2:]


def early_kernel(count, *refs):
    factors, parts, out_ref = refs[:count], refs[count : 2 * count], refs[2 * count]
    at = 0
    for f, p in zip(factors, parts):
        depth, width = p.shape
        out_ref[:, at : at + width] = jnp.dot(
            f[:, :depth], p[...], preferred_element_type=F32
        )
        at += width


def late_kernel(count, row, *refs):
    factors, parts, sum_ref, out_ref = (
        refs[:count],
        refs[count : 2 * count],
        refs[2 * count],
        refs[2 * count + 1],
    )
    rows = out_ref.shape[0]
    at = 0
    for f, p in zip(factors, parts):
        depth, width = p.shape
        product = jnp.dot(f[row : row + rows, depth:], p[...], preferred_element_type=F32)
        out_ref[:, at : at + width] = (
            sum_ref[row : row + rows, at : at + width] + product
        ).astype(out_ref.dtype)
        at += width


def body(activations, grad_output, projector, first_moment, second_moment):
    place = lax.axis_index("fsdp").astype(jnp.int32)
    tp_place = lax.axis_index("tp").astype(jnp.int32)
    core = place & 1
    chip = place >> 1
    tokens, width = grad_output.shape
    half = width // 2
    rank = projector.shape[1]
    block = rank // 16
    column_count = rank // 8
    wide = half * 3 // 7
    widths = (wide, wide, half - 2 * wide)
    rows = first_moment.shape[0]

    def my_half(array):
        return lax.dynamic_slice_in_dim(array, core * half, half, 1)

    def other_half(array):
        return lax.dynamic_slice_in_dim(array, (1 - core) * half, half, 1)

    columns = lax.dynamic_slice_in_dim(projector, tp_place * column_count, column_count, 1)
    columns = stack([[columns] + [swap(columns, "fsdp", m) for m in (8, 16, 24)]])[0]
    columns = stack([[columns] + [swap(columns, "fsdp", m) for m in (2, 4, 6)]])[0]
    columns_other = swap(columns, "fsdp", 1)
    order = [x + z for x in (0, 2, 4, 6) for z in (0, 8, 16, 24)]
    index = jnp.concatenate([place ^ c ^ table(order) for c in range(2)])
    act = reorder(activations, index, projector.shape[0])
    depth = columns.shape[0]
    dims = (((0,), (1,)), ((), ()))
    own = lax.dot_general(columns, act[:, :depth], dims, preferred_element_type=F32)
    own = own + lax.dot_general(columns_other, act[:, depth:], dims, preferred_element_type=F32)
    own = own.astype(BF)

    coords = stack([[own, swap(own, "tp", 1)]])[0]
    coords = stack([[coords] + [swap(coords, "tp", m) for m in (2, 4, 6)]])[0]
    coords_other = swap(coords, "fsdp", 1)

    grads = jnp.concatenate(
        [my_half(grad_output), swap(other_half(grad_output), "fsdp", 1)], axis=0
    )
    moments = jnp.concatenate([first_moment, second_moment], axis=0)
    moments_other = swap(other_half(moments), "fsdp", 1)
    moments_own = my_half(moments)
    first = by_core(core, moments_own[:rows], moments_other[:rows], 0)
    second = by_core(core, moments_own[rows:], moments_other[rows:], 0)
    both = jnp.concatenate([projector, swap(projector, "fsdp", 1)], axis=0)

    sum_orders = ([1, 3, 4, 12], [3, 1, 12, 4], [4, 12, 1, 3])
    keep_index, send_index = [], []
    for masks in sum_orders:
        wanted = chip ^ table(doubled(masks[::-1]))
        position = 2 * (tp_place ^ (wanted >> 1)) + (wanted & 1)
        keep_index.append(position[:8])
        send_index.append(position[8:])
    back_orders = [m[::-1] for m in sum_orders]
    ranks = jnp.arange(rank, dtype=jnp.int32)
    factors = []
    for masks in back_orders:
        blocks = chip ^ table(doubled(masks))
        wanted = (blocks[:, None] * block + ranks[None, :block]).reshape(-1)
        choose = (ranks[:, None] == wanted[None, :]).astype(BF)
        factors.append(jnp.dot(both, choose, preferred_element_type=F32).astype(BF))
    arrays = (coords, coords_other, grads, rank // 2, widths, block)
    sent = partial_sums(jnp.concatenate(send_index), *arrays, BF)
    kept = partial_sums(jnp.concatenate(keep_index), *arrays, F32, after=factors)
    for stage in range(3):
        got = [swap(s, "fsdp", 2 * m[stage]) for s, m in zip(sent, sum_orders)]
        kept, sent = halve(kept, got)
    got = [swap(s, "fsdp", 2 * m[3]) for s, m in zip(sent, sum_orders)]
    new_first, new_second, parts = adam(kept, got, first, second)

    def rows_of(array, which):
        return lax.dynamic_slice_in_dim(array, which * rows, rows, 0)

    states_other = swap(
        jnp.concatenate([rows_of(new_first, 1 - core), rows_of(new_second, 1 - core)], axis=0),
        "fsdp",
        1,
    )
    out_first = by_core(core, rows_of(new_first, core), states_other[:rows], 1)
    out_second = by_core(core, rows_of(new_second, core), states_other[rows:], 1)

    for stage in range(4):
        got = [swap(p, "fsdp", 2 * m[stage]) for p, m in zip(parts, back_orders)]
        if stage < 3:
            parts = stack([[p, g] for p, g in zip(parts, got)])
    count = len(parts)
    flops = rank * half * both.shape[0]
    early = call(
        functools.partial(early_kernel, count),
        [shape(both.shape[0], half, F32)],
        [*factors, *parts],
        flops=flops,
        vmem=32,
    )[0]
    late = [
        call(
            functools.partial(late_kernel, count, row),
            [shape(tokens, half, BF)],
            [*factors, *got, early],
            flops=flops // 2,
            vmem=32,
        )[0]
        for row in (tokens, 0)
    ]
    update = by_core(core, late[1], swap(late[0], "fsdp", 1), 1)
    return (out_first, out_second, update)


def solution(mesh):
    return jax.shard_map(
        body,
        mesh=mesh,
        in_specs=(
            P("fsdp", None),
            P("fsdp", "tp"),
            P("fsdp", None),
            P("fsdp", "tp"),
            P("fsdp", "tp"),
        ),
        out_specs=(P("fsdp", "tp"), P("fsdp", "tp"), P("fsdp", "tp")),
        check_vma=False,
    )
```

profile of v0, /device:TPU:1, one launch (start us, length us, event | category | flops | bytes accessed | tf_op | source)
XLA Modules:
  0.0 181.7 jit_solution(10438718733255749930)
XLA Ops:
  1.5 3.8 %collective-permute-start = (bf16[256,128]{1,0:T(8,128)(2,1)S(1)}, bf16[256,128]{1,0:T(8,128)(2,1)S(1)}, u32[]{:S(2)}, u32[]{:S(2)}) collective-permute-start(bf16[256,128]{1,0:T(8,128)(2,1)S(1)} %constant_dynamic-slice_fusion.8.refs_0_), channel_id=1, source_target_pairs={{0,64},{8,72},{16,80},{24,88},{32,96},{40,104},{48,112},{56,120},{... | collective-permute-start | bytes 196616 | tf_op jit(solution)/shard_map/ppermute | solution.py:19
  5.4 5.1 %collective-permute-start.1 = (bf16[256,128]{1,0:T(8,128)(2,1)S(1)}, bf16[256,128]{1,0:T(8,128)(2,1)S(1)}, u32[]{:S(2)}, u32[]{:S(2)}) collective-permute-start(bf16[256,128]{1,0:T(8,128)(2,1)S(1)} %constant_dynamic-slice_fusion.8.refs_0_), channel_id=1, source_target_pairs={{0,128},{8,136},{16,144},{24,152},{32,160},{40,168},{48,176},{56,1... | collective-permute-start | bytes 196616 | tf_op jit(solution)/shard_map/ppermute | solution.py:19
  10.5 1.2 collective-permute-start.13
  11.7 2.5 %constant_dynamic-slice_fusion.7 = (bf16[256,1792]{1,0:T(8,128)(2,1)S(1)}, bf16[256,1792]{1,0:T(8,128)(2,1)}) fusion(bf16[256,3584]{1,0:T(8,128)(2,1)} %param.14, s32[]{:T(128)S(6)} %select_n.53, s32[]{:T(128)S(6)} %select_n.54), kind=kLoop, calls=%fused_computation.39 | loop fusion | bytes 3670024 | tf_op jit(solution)/shard_map/dynamic_slice | solution.py:218
  16.0 1.3 collective-permute-start.3
  17.3 2.5 %collective-permute-start.4 = (bf16[1024,128]{1,0:T(8,128)(2,1)S(1)}, bf16[1024,128]{1,0:T(8,128)(2,1)S(1)}, u32[]{:S(2)}, u32[]{:S(2)}) collective-permute-start(bf16[1024,128]{1,0:T(8,128)(2,1)S(1)} %shard_map.148.refs_0_), channel_id=1, source_target_pairs={{0,32},{8,40},{16,48},{24,56},{32,0},{40,8},{48,16},{56,24},{64,96... | collective-permute-start | bytes 786440 | tf_op jit(solution)/shard_map/ppermute | solution.py:19
  20.0 2.2 %copy-done = bf16[256,8192]{1,0:T(8,128)(2,1)S(1)} copy-done((bf16[256,8192]{1,0:T(8,128)(2,1)S(1)}, bf16[256,8192]{1,0:T(8,128)(2,1)}, u32[]{:S(2)}) %copy-start) | copy-done | bytes 4194328
  24.0 5.5 %collective-permute-done.4.refs_2_ = bf16[1024,128]{1,0:T(8,128)(2,1)S(1)} collective-permute-done((bf16[1024,128]{1,0:T(8,128)(2,1)S(1)}, bf16[1024,128]{1,0:T(8,128)(2,1)S(1)}, u32[]{:S(2)}, u32[]{:S(2)}) %collective-permute-start.4) | collective-permute-done | bytes 262176 | tf_op jit(solution)/shard_map/ppermute | solution.py:19
  29.6 3.5 %collective-permute-done.5.refs_3_ = bf16[1024,128]{1,0:T(8,128)(2,1)S(1)} collective-permute-done((bf16[1024,128]{1,0:T(8,128)(2,1)S(1)}, bf16[1024,128]{1,0:T(8,128)(2,1)S(1)}, u32[]{:S(2)}, u32[]{:S(2)}) %collective-permute-start.5) | collective-permute-done | bytes 262176 | tf_op jit(solution)/shard_map/ppermute | solution.py:19
  33.2 2.3 %collective-permute-start.6 = (bf16[4096,128]{1,0:T(8,128)(2,1)S(1)}, bf16[4096,128]{1,0:T(8,128)(2,1)S(1)}, u32[]{:S(2)}, u32[]{:S(2)}) collective-permute-start(bf16[4096,128]{1,0:T(8,128)(2,1)S(1)} %shard_map.149), channel_id=1, source_target_pairs={{0,8},{8,0},{16,24},{24,16},{32,40},{40,32},{48,56},{56,48},{64,72... | collective-permute-start | bytes 3145736 | tf_op jit(solution)/shard_map/ppermute | solution.py:19
  36.5 1.3 collective-permute-done.6
  40.9 1.8 collective-permute-done.7.refs_1_
  42.6 2.8 %collective-permute-start.10 = (bf16[256,256]{1,0:T(8,128)(2,1)S(1)}, bf16[256,256]{1,0:T(8,128)(2,1)S(1)}, u32[]{:S(2)}, u32[]{:S(2)}) collective-permute-start(bf16[256,256]{1,0:T(8,128)(2,1)S(1)} %shard_map.151.refs_0_), channel_id=1, source_target_pairs={{0,6},{1,7},{2,4},{3,5},{4,2},{5,3},{6,0},{7,1},{8,14},{9,15},{10,... | collective-permute-start | bytes 393224 | tf_op jit(solution)/shard_map/ppermute | solution.py:19
  45.5 1.3 collective-permute-start.9
  49.1 2.2 %collective-permute-start.26 = (f32[64,1792]{1,0:T(8,128)}, f32[64,1792]{1,0:T(8,128)}, u32[]{:S(2)}, u32[]{:S(2)}) collective-permute-start(f32[64,1792]{1,0:T(8,128)} %constant_dynamic-slice_fusion.5), channel_id=1, source_target_pairs={{0,8},{8,0},{16,24},{24,16},{32,40},{40,32},{48,56},{56,48},{64,72... | collective-permute-start | bytes 1376264 | tf_op jit(solution)/shard_map/ppermute | solution.py:19
  51.9 2.5 %collective-permute-start.11 = (bf16[1024,256]{1,0:T(8,128)(2,1)S(1)}, bf16[1024,256]{1,0:T(8,128)(2,1)S(1)}, u32[]{:S(2)}, u32[]{:S(2)}) collective-permute-start(bf16[1024,256]{1,0:T(8,128)(2,1)S(1)} %shard_map.152.refs_1_), channel_id=1, source_target_pairs={{0,8},{8,0},{16,24},{24,16},{32,40},{40,32},{48,56},{56,48},{64,72... | collective-permute-start | bytes 1572872 | tf_op jit(solution)/shard_map/ppermute | solution.py:19
  54.6 1.3 collective-permute-done.11.refs_2_
  55.9 1.7 shard_map.154
  58.2 1.3 fusion.10.refs_6_.refs_2_
  59.5 1.3 fusion.11.refs_5_.refs_1_
  61.9 1.3 fusion.12.refs_4_.refs_0_
  63.2 1.7 shard_map.153
  64.9 10.3 %collective-permute-done.16.refs_5_ = bf16[512,256]{1,0:T(8,128)(2,1)S(1)} collective-permute-done((bf16[512,256]{1,0:T(8,128)(2,1)S(1)}, bf16[512,256]{1,0:T(8,128)(2,1)S(1)}, u32[]{:S(2)}, u32[]{:S(2)}) %collective-permute-start.16) | collective-permute-done | bytes 262176 | tf_op jit(solution)/shard_map/ppermute | solution.py:19
  75.1 1.5 collective-permute-done.14.refs_3_
  76.6 1.3 collective-permute-done.15.refs_4_
  82.4 4.3 %collective-permute-start.19 = (bf16[256,256]{1,0:T(8,128)(2,1)}, bf16[256,256]{1,0:T(8,128)(2,1)S(1)}, u32[]{:S(2)}, u32[]{:S(2)}) collective-permute-start(bf16[256,256]{1,0:T(8,128)(2,1)} %copy-done.7), channel_id=1, source_target_pairs={{0,192},{8,200},{16,208},{24,216},{32,224},{40,232},{48,240},{56,2... | collective-permute-start | bytes 393224 | tf_op jit(solution)/shard_map/ppermute | solution.py:19
  87.9 4.4 %collective-permute-done.19.refs_5_ = bf16[256,256]{1,0:T(8,128)(2,1)S(1)} collective-permute-done((bf16[256,256]{1,0:T(8,128)(2,1)}, bf16[256,256]{1,0:T(8,128)(2,1)S(1)}, u32[]{:S(2)}, u32[]{:S(2)}) %collective-permute-start.19) | collective-permute-done | bytes 131104 | tf_op jit(solution)/shard_map/ppermute | solution.py:19
  98.6 4.6 %collective-permute-start.21 = (bf16[128,768]{1,0:T(8,128)(2,1)S(1)}, bf16[128,768]{1,0:T(8,128)(2,1)S(1)}, u32[]{:S(2)}, u32[]{:S(2)}) collective-permute-start(bf16[128,768]{1,0:T(8,128)(2,1)S(1)} %get-tuple-element.57), channel_id=1, source_target_pairs={{0,192},{8,200},{16,208},{24,216},{32,224},{40,232},{48,240},{56,2... | collective-permute-start | bytes 589832 | tf_op jit(solution)/shard_map/ppermute | solution.py:19
  104.3 2.3 %collective-permute-done.22.refs_5_ = bf16[128,256]{1,0:T(8,128)(2,1)S(1)} collective-permute-done((bf16[128,256]{1,0:T(8,128)(2,1)S(1)}, bf16[128,256]{1,0:T(8,128)(2,1)S(1)}, u32[]{:S(2)}, u32[]{:S(2)}) %collective-permute-start.22) | collective-permute-done | bytes 65568 | tf_op jit(solution)/shard_map/ppermute | solution.py:19
  106.7 2.3 %collective-permute-done.20.refs_3_ = bf16[128,768]{1,0:T(8,128)(2,1)S(1)} collective-permute-done((bf16[128,768]{1,0:T(8,128)(2,1)S(1)}, bf16[128,768]{1,0:T(8,128)(2,1)S(1)}, u32[]{:S(2)}, u32[]{:S(2)}) %collective-permute-start.20) | collective-permute-done | bytes 196640 | tf_op jit(solution)/shard_map/ppermute | solution.py:19
  109.1 2.1 %collective-permute-start.23 = (bf16[64,768]{1,0:T(8,128)(2,1)S(1)}, bf16[64,768]{1,0:T(8,128)(2,1)S(1)}, u32[]{:S(2)}, u32[]{:S(2)}) collective-permute-start(bf16[64,768]{1,0:T(8,128)(2,1)S(1)} %get-tuple-element.62), channel_id=1, source_target_pairs={{0,192},{8,200},{16,208},{24,216},{32,224},{40,232},{48,240},{56,2... | collective-permute-start | bytes 294920 | tf_op jit(solution)/shard_map/ppermute | solution.py:19
  111.2 5.1 %collective-permute-start.24 = (bf16[64,768]{1,0:T(8,128)(2,1)S(1)}, bf16[64,768]{1,0:T(8,128)(2,1)S(1)}, u32[]{:S(2)}, u32[]{:S(2)}) collective-permute-start(bf16[64,768]{1,0:T(8,128)(2,1)S(1)} %get-tuple-element.63), channel_id=1, source_target_pairs={{0,64},{8,72},{16,80},{24,88},{32,96},{40,104},{48,112},{56,120},{... | collective-permute-start | bytes 294920 | tf_op jit(solution)/shard_map/ppermute | solution.py:19
  116.3 1.6 collective-permute-start.25
  117.9 2.6 %collective-permute-done.25.refs_5_ = bf16[64,256]{1,0:T(8,128)(2,1)S(1)} collective-permute-done((bf16[64,256]{1,0:T(8,128)(2,1)S(1)}, bf16[64,256]{1,0:T(8,128)(2,1)S(1)}, u32[]{:S(2)}, u32[]{:S(2)}) %collective-permute-start.25) | collective-permute-done | bytes 32800 | tf_op jit(solution)/shard_map/ppermute | solution.py:19
  121.3 2.7 %collective-permute-start.29 = (bf16[64,768]{1,0:T(8,128)(2,1)S(1)}, bf16[64,768]{1,0:T(8,128)(2,1)S(1)}, u32[]{:S(2)}, u32[]{:S(2)}) collective-permute-start(bf16[64,768]{1,0:T(8,128)(2,1)S(1)} %get-tuple-element.68.refs_2_), channel_id=1, source_target_pairs={{0,64},{8,72},{16,80},{24,88},{32,96},{40,104},{48,112},{56,120},{... | collective-permute-start | bytes 294920 | tf_op jit(solution)/shard_map/ppermute | solution.py:19
  124.3 3.6 %collective-permute-done.30.refs_5_ = bf16[64,256]{1,0:T(8,128)(2,1)S(1)} collective-permute-done((bf16[64,256]{1,0:T(8,128)(2,1)S(1)}, bf16[64,256]{1,0:T(8,128)(2,1)S(1)}, u32[]{:S(2)}, u32[]{:S(2)}) %collective-permute-start.30) | collective-permute-done | bytes 32800 | tf_op jit(solution)/shard_map/ppermute | solution.py:19
  128.6 3.0 %collective-permute-start.32 = (bf16[128,768]{1,0:T(8,128)(2,1)S(1)}, bf16[128,768]{1,0:T(8,128)(2,1)S(1)}, u32[]{:S(2)}, u32[]{:S(2)}) collective-permute-start(bf16[128,768]{1,0:T(8,128)(2,1)S(1)} %get-tuple-element.71.refs_2_), channel_id=1, source_target_pairs={{0,192},{8,200},{16,208},{24,216},{32,224},{40,232},{48,240},{56,2... | collective-permute-start | bytes 589832 | tf_op jit(solution)/shard_map/ppermute | solution.py:19
  131.8 3.0 %collective-permute-done.33.refs_5_ = bf16[128,256]{1,0:T(8,128)(2,1)S(1)} collective-permute-done((bf16[128,256]{1,0:T(8,128)(2,1)S(1)}, bf16[128,256]{1,0:T(8,128)(2,1)S(1)}, u32[]{:S(2)}, u32[]{:S(2)}) %collective-permute-start.33) | collective-permute-done | bytes 65568 | tf_op jit(solution)/shard_map/ppermute | solution.py:19
  136.8 3.4 %collective-permute-start.35 = (bf16[256,768]{1,0:T(8,128)(2,1)S(1)}, bf16[256,768]{1,0:T(8,128)(2,1)S(1)}, u32[]{:S(2)}, u32[]{:S(2)}) collective-permute-start(bf16[256,768]{1,0:T(8,128)(2,1)S(1)} %get-tuple-element.74.refs_2_), channel_id=1, source_target_pairs={{0,16},{8,24},{16,0},{24,8},{32,48},{40,56},{48,32},{56,40},{64,80... | collective-permute-start | bytes 1179656 | tf_op jit(solution)/shard_map/ppermute | solution.py:19
  140.2 5.1 %collective-permute-start.27 = (f32[64,1792]{1,0:T(8,128)S(1)}, f32[64,1792]{1,0:T(8,128)S(1)}, u32[]{:S(2)}, u32[]{:S(2)}) collective-permute-start(f32[64,1792]{1,0:T(8,128)S(1)} %pad_maximum_fusion.1), channel_id=1, source_target_pairs={{0,8},{8,0},{16,24},{24,16},{32,40},{40,32},{48,56},{56,48},{64,72... | collective-permute-start | bytes 1376264 | tf_op jit(solution)/shard_map/ppermute | solution.py:19
  145.4 3.1 %collective-permute-start.36 = (bf16[256,256]{1,0:T(8,128)(2,1)S(1)}, bf16[256,256]{1,0:T(8,128)(2,1)S(1)}, u32[]{:S(2)}, u32[]{:S(2)}) collective-permute-start(bf16[256,256]{1,0:T(8,128)(2,1)S(1)} %get-tuple-element.75.refs_4_), channel_id=1, source_target_pairs={{0,192},{8,200},{16,208},{24,216},{32,224},{40,232},{48,240},{56,2... | collective-permute-start | bytes 393224 | tf_op jit(solution)/shard_map/ppermute | solution.py:19
  148.4 5.5 %collective-permute-done.36.refs_5_ = bf16[256,256]{1,0:T(8,128)(2,1)S(1)} collective-permute-done((bf16[256,256]{1,0:T(8,128)(2,1)S(1)}, bf16[256,256]{1,0:T(8,128)(2,1)S(1)}, u32[]{:S(2)}, u32[]{:S(2)}) %collective-permute-start.36) | collective-permute-done | bytes 131104 | tf_op jit(solution)/shard_map/ppermute | solution.py:19
  154.1 1.8 collective-permute-start.37
  157.1 3.6 %collective-permute-start.39 = (bf16[512,256]{1,0:T(8,128)(2,1)S(1)}, bf16[512,256]{1,0:T(8,128)(2,1)S(1)}, u32[]{:S(2)}, u32[]{:S(2)}) collective-permute-start(bf16[512,256]{1,0:T(8,128)(2,1)S(1)} %get-tuple-element.78.refs_5_), channel_id=1, source_target_pairs={{0,64},{8,72},{16,80},{24,88},{32,96},{40,104},{48,112},{56,120},{... | collective-permute-start | bytes 786440 | tf_op jit(solution)/shard_map/ppermute | solution.py:19
  161.9 11.0 %collective-permute-done.39.refs_5_ = bf16[512,256]{1,0:T(8,128)(2,1)S(1)} collective-permute-done((bf16[512,256]{1,0:T(8,128)(2,1)S(1)}, bf16[512,256]{1,0:T(8,128)(2,1)S(1)}, u32[]{:S(2)}, u32[]{:S(2)}) %collective-permute-start.39) | collective-permute-done | bytes 262176 | tf_op jit(solution)/shard_map/ppermute | solution.py:19
  172.9 2.5 %collective-permute-done.38.refs_4_ = bf16[512,768]{1,0:T(8,128)(2,1)S(1)} collective-permute-done((bf16[512,768]{1,0:T(8,128)(2,1)S(1)}, bf16[512,768]{1,0:T(8,128)(2,1)S(1)}, u32[]{:S(2)}, u32[]{:S(2)}) %collective-permute-start.38) | collective-permute-done | bytes 786464 | tf_op jit(solution)/shard_map/ppermute | solution.py:19
  176.1 1.7 collective-permute-start.40
  180.0 1.6 maximum_select_fusion
  (123 shorter events, 36.1 us)
Async XLA Ops:
  0.6 13.6 %copy-start.15 = (s32[16]{0:T(128)S(1)}, s32[16]{0:T(128)}, u32[]{:S(2)}) copy-start(s32[16]{0:T(128)} %constant.39.clone) | copy-start | bytes 196
  0.6 13.6 %copy-start.16 = (s32[16]{0:T(128)S(1)}, s32[16]{0:T(128)}, u32[]{:S(2)}) copy-start(s32[16]{0:T(128)} %constant.40.clone) | copy-start | bytes 196
  0.7 14.7 %copy-start.14 = (s32[16]{0:T(128)S(1)}, s32[16]{0:T(128)}, u32[]{:S(2)}) copy-start(s32[16]{0:T(128)} %constant.38.clone) | copy-start | bytes 196
  0.7 14.7 %copy-start.13 = (s32[16]{0:T(128)S(1)}, s32[16]{0:T(128)}, u32[]{:S(2)}) copy-start(s32[16]{0:T(128)} %constant.37.clone) | copy-start | bytes 196
  1.5 13.9 %collective-permute-start = (bf16[256,128]{1,0:T(8,128)(2,1)S(1)}, bf16[256,128]{1,0:T(8,128)(2,1)S(1)}, u32[]{:S(2)}, u32[]{:S(2)}) collective-permute-start(bf16[256,128]{1,0:T(8,128)(2,1)S(1)} %constant_dynamic-slice_fusion.8.refs_0_), channel_id=1, source_target_pairs={{0,64},{8,72},{16,80},{24,88},{32,96},{40,104},{48,112},{56,120},{... | collective-permute-start | bytes 196616 | tf_op jit(solution)/shard_map/ppermute | solution.py:19
  5.4 10.1 %collective-permute-start.1 = (bf16[256,128]{1,0:T(8,128)(2,1)S(1)}, bf16[256,128]{1,0:T(8,128)(2,1)S(1)}, u32[]{:S(2)}, u32[]{:S(2)}) collective-permute-start(bf16[256,128]{1,0:T(8,128)(2,1)S(1)} %constant_dynamic-slice_fusion.8.refs_0_), channel_id=1, source_target_pairs={{0,128},{8,136},{16,144},{24,152},{32,160},{40,168},{48,176},{56,1... | collective-permute-start | bytes 196616 | tf_op jit(solution)/shard_map/ppermute | solution.py:19
  10.5 5.5 %collective-permute-start.2 = (bf16[256,128]{1,0:T(8,128)(2,1)S(1)}, bf16[256,128]{1,0:T(8,128)(2,1)S(1)}, u32[]{:S(2)}, u32[]{:S(2)}) collective-permute-start(bf16[256,128]{1,0:T(8,128)(2,1)S(1)} %constant_dynamic-slice_fusion.8.refs_0_), channel_id=1, source_target_pairs={{0,192},{8,200},{16,208},{24,216},{32,224},{40,232},{48,240},{56,2... | collective-permute-start | bytes 196616 | tf_op jit(solution)/shard_map/ppermute | solution.py:19
  10.5 44.0 %collective-permute-start.13 = (bf16[256,1024]{1,0:T(8,128)(2,1)}, bf16[256,1024]{1,0:T(8,128)(2,1)S(1)}, u32[]{:S(2)}, u32[]{:S(2)}) collective-permute-start(bf16[256,1024]{1,0:T(8,128)(2,1)} %param.15), channel_id=1, source_target_pairs={{0,8},{8,0},{16,24},{24,16},{32,40},{40,32},{48,56},{56,48},{64,72... | collective-permute-start | bytes 1572872 | tf_op jit(solution)/shard_map/ppermute | solution.py:19
  14.2 40.3 %collective-permute-start.12 = (bf16[256,1792]{1,0:T(8,128)(2,1)}, bf16[256,1792]{1,0:T(8,128)(2,1)S(1)}, u32[]{:S(2)}, u32[]{:S(2)}) collective-permute-start(bf16[256,1792]{1,0:T(8,128)(2,1)} %get-tuple-element.80), channel_id=1, source_target_pairs={{0,8},{8,0},{16,24},{24,16},{32,40},{40,32},{48,56},{56,48},{64,72... | collective-permute-start | bytes 2752520 | tf_op jit(solution)/shard_map/ppermute | solution.py:19
  16.0 8.1 %collective-permute-start.3 = (bf16[1024,128]{1,0:T(8,128)(2,1)S(1)}, bf16[1024,128]{1,0:T(8,128)(2,1)S(1)}, u32[]{:S(2)}, u32[]{:S(2)}) collective-permute-start(bf16[1024,128]{1,0:T(8,128)(2,1)S(1)} %shard_map.148.refs_0_), channel_id=1, source_target_pairs={{0,16},{8,24},{16,0},{24,8},{32,48},{40,56},{48,32},{56,40},{64,80... | collective-permute-start | bytes 786440 | tf_op jit(solution)/shard_map/ppermute | solution.py:19
  17.3 12.3 %collective-permute-start.4 = (bf16[1024,128]{1,0:T(8,128)(2,1)S(1)}, bf16[1024,128]{1,0:T(8,128)(2,1)S(1)}, u32[]{:S(2)}, u32[]{:S(2)}) collective-permute-start(bf16[1024,128]{1,0:T(8,128)(2,1)S(1)} %shard_map.148.refs_0_), channel_id=1, source_target_pairs={{0,32},{8,40},{16,48},{24,56},{32,0},{40,8},{48,16},{56,24},{64,96... | collective-permute-start | bytes 786440 | tf_op jit(solution)/shard_map/ppermute | solution.py:19
  19.7 13.4 %collective-permute-start.5 = (bf16[1024,128]{1,0:T(8,128)(2,1)S(1)}, bf16[1024,128]{1,0:T(8,128)(2,1)S(1)}, u32[]{:S(2)}, u32[]{:S(2)}) collective-permute-start(bf16[1024,128]{1,0:T(8,128)(2,1)S(1)} %shard_map.148.refs_0_), channel_id=1, source_target_pairs={{0,48},{8,56},{16,32},{24,40},{32,16},{40,24},{48,0},{56,8},{64,11... | collective-permute-start | bytes 786440 | tf_op jit(solution)/shard_map/ppermute | solution.py:19
  23.3 12.1 %copy-start.10 = (f32[32,3584]{1,0:T(8,128)S(1)}, f32[32,3584]{1,0:T(8,128)}, u32[]{:S(2)}) copy-start(f32[32,3584]{1,0:T(8,128)} %param.16) | copy-start | bytes 1376260
  23.4 12.1 %copy-start.11 = (f32[32,3584]{1,0:T(8,128)S(1)}, f32[32,3584]{1,0:T(8,128)}, u32[]{:S(2)}) copy-start(f32[32,3584]{1,0:T(8,128)} %param.17) | copy-start | bytes 1376260
  33.2 4.6 %collective-permute-start.6 = (bf16[4096,128]{1,0:T(8,128)(2,1)S(1)}, bf16[4096,128]{1,0:T(8,128)(2,1)S(1)}, u32[]{:S(2)}, u32[]{:S(2)}) collective-permute-start(bf16[4096,128]{1,0:T(8,128)(2,1)S(1)} %shard_map.149), channel_id=1, source_target_pairs={{0,8},{8,0},{16,24},{24,16},{32,40},{40,32},{48,56},{56,48},{64,72... | collective-permute-start | bytes 3145736 | tf_op jit(solution)/shard_map/ppermute | solution.py:19
  38.6 15.8 %copy-start.9 = (bf16[256,1024]{1,0:T(8,128)(2,1)S(1)}, bf16[256,1024]{1,0:T(8,128)(2,1)}, u32[]{:S(2)}) copy-start(bf16[256,1024]{1,0:T(8,128)(2,1)} %param.15) | copy-start | bytes 1572868
  39.4 3.2 %collective-permute-start.7 = (bf16[128,256]{1,0:T(8,128)(2,1)S(1)}, bf16[128,256]{1,0:T(8,128)(2,1)S(1)}, u32[]{:S(2)}, u32[]{:S(2)}) collective-permute-start(bf16[128,256]{1,0:T(8,128)(2,1)S(1)} %fusion.16.refs_0_), channel_id=1, source_target_pairs={{0,1},{1,0},{2,3},{3,2},{4,5},{5,4},{6,7},{7,6},{8,9},{9,8},{10,11... | collective-permute-start | bytes 196616 | tf_op jit(solution)/shard_map/ppermute | solution.py:19
  42.6 6.4 %collective-permute-start.10 = (bf16[256,256]{1,0:T(8,128)(2,1)S(1)}, bf16[256,256]{1,0:T(8,128)(2,1)S(1)}, u32[]{:S(2)}, u32[]{:S(2)}) collective-permute-start(bf16[256,256]{1,0:T(8,128)(2,1)S(1)} %shard_map.151.refs_0_), channel_id=1, source_target_pairs={{0,6},{1,7},{2,4},{3,5},{4,2},{5,3},{6,0},{7,1},{8,14},{9,15},{10,... | collective-permute-start | bytes 393224 | tf_op jit(solution)/shard_map/ppermute | solution.py:19
  45.5 5.9 %collective-permute-start.8 = (bf16[256,256]{1,0:T(8,128)(2,1)S(1)}, bf16[256,256]{1,0:T(8,128)(2,1)S(1)}, u32[]{:S(2)}, u32[]{:S(2)}) collective-permute-start(bf16[256,256]{1,0:T(8,128)(2,1)S(1)} %shard_map.151.refs_0_), channel_id=1, source_target_pairs={{0,2},{1,3},{2,0},{3,1},{4,6},{5,7},{6,4},{7,5},{8,10},{9,11},{10,... | collective-permute-start | bytes 393224 | tf_op jit(solution)/shard_map/ppermute | solution.py:19
  45.5 6.4 %collective-permute-start.9 = (bf16[256,256]{1,0:T(8,128)(2,1)S(1)}, bf16[256,256]{1,0:T(8,128)(2,1)S(1)}, u32[]{:S(2)}, u32[]{:S(2)}) collective-permute-start(bf16[256,256]{1,0:T(8,128)(2,1)S(1)} %shard_map.151.refs_0_), channel_id=1, source_target_pairs={{0,4},{1,5},{2,6},{3,7},{4,0},{5,1},{6,2},{7,3},{8,12},{9,13},{10,... | collective-permute-start | bytes 393224 | tf_op jit(solution)/shard_map/ppermute | solution.py:19
  49.1 54.2 %collective-permute-start.26 = (f32[64,1792]{1,0:T(8,128)}, f32[64,1792]{1,0:T(8,128)}, u32[]{:S(2)}, u32[]{:S(2)}) collective-permute-start(f32[64,1792]{1,0:T(8,128)} %constant_dynamic-slice_fusion.5), channel_id=1, source_target_pairs={{0,8},{8,0},{16,24},{24,16},{32,40},{40,32},{48,56},{56,48},{64,72... | collective-permute-start | bytes 1376264 | tf_op jit(solution)/shard_map/ppermute | solution.py:19
  51.9 4.1 %collective-permute-start.11 = (bf16[1024,256]{1,0:T(8,128)(2,1)S(1)}, bf16[1024,256]{1,0:T(8,128)(2,1)S(1)}, u32[]{:S(2)}, u32[]{:S(2)}) collective-permute-start(bf16[1024,256]{1,0:T(8,128)(2,1)S(1)} %shard_map.152.refs_1_), channel_id=1, source_target_pairs={{0,8},{8,0},{16,24},{24,16},{32,40},{40,32},{48,56},{56,48},{64,72... | collective-permute-start | bytes 1572872 | tf_op jit(solution)/shard_map/ppermute | solution.py:19
  57.6 19.0 %collective-permute-start.14 = (bf16[512,768]{1,0:T(8,128)(2,1)S(1)}, bf16[512,768]{1,0:T(8,128)(2,1)S(1)}, u32[]{:S(2)}, u32[]{:S(2)}) collective-permute-start(bf16[512,768]{1,0:T(8,128)(2,1)S(1)} %get-tuple-element.44), channel_id=1, source_target_pairs={{0,16},{8,24},{16,0},{24,8},{32,48},{40,56},{48,32},{56,40},{64,80... | collective-permute-start | bytes 2359304 | tf_op jit(solution)/shard_map/ppermute | solution.py:19
  57.9 20.1 %collective-permute-start.15 = (bf16[512,768]{1,0:T(8,128)(2,1)S(1)}, bf16[512,768]{1,0:T(8,128)(2,1)S(1)}, u32[]{:S(2)}, u32[]{:S(2)}) collective-permute-start(bf16[512,768]{1,0:T(8,128)(2,1)S(1)} %get-tuple-element.45), channel_id=1, source_target_pairs={{0,48},{8,56},{16,32},{24,40},{32,16},{40,24},{48,0},{56,8},{64,11... | collective-permute-start | bytes 2359304 | tf_op jit(solution)/shard_map/ppermute | solution.py:19
  60.8 14.3 %collective-permute-start.16 = (bf16[512,256]{1,0:T(8,128)(2,1)S(1)}, bf16[512,256]{1,0:T(8,128)(2,1)S(1)}, u32[]{:S(2)}, u32[]{:S(2)}) collective-permute-start(bf16[512,256]{1,0:T(8,128)(2,1)S(1)} %get-tuple-element.46), channel_id=1, source_target_pairs={{0,64},{8,72},{16,80},{24,88},{32,96},{40,104},{48,112},{56,120},{... | collective-permute-start | bytes 786440 | tf_op jit(solution)/shard_map/ppermute | solution.py:19
  82.2 10.8 %collective-permute-start.17 = (bf16[256,768]{1,0:T(8,128)(2,1)}, bf16[256,768]{1,0:T(8,128)(2,1)S(1)}, u32[]{:S(2)}, u32[]{:S(2)}) collective-permute-start(bf16[256,768]{1,0:T(8,128)(2,1)} %get-tuple-element.50), channel_id=1, source_target_pairs={{0,48},{8,56},{16,32},{24,40},{32,16},{40,24},{48,0},{56,8},{64,11... | collective-permute-start | bytes 1179656 | tf_op jit(solution)/shard_map/ppermute | solution.py:19
  82.4 10.6 %collective-permute-start.18 = (bf16[256,768]{1,0:T(8,128)(2,1)}, bf16[256,768]{1,0:T(8,128)(2,1)}, u32[]{:S(2)}, u32[]{:S(2)}) collective-permute-start(bf16[256,768]{1,0:T(8,128)(2,1)} %get-tuple-element.51), channel_id=1, source_target_pairs={{0,16},{8,24},{16,0},{24,8},{32,48},{40,56},{48,32},{56,40},{64,80... | collective-permute-start | bytes 1179656 | tf_op jit(solution)/shard_map/ppermute | solution.py:19
  82.4 9.8 %collective-permute-start.19 = (bf16[256,256]{1,0:T(8,128)(2,1)}, bf16[256,256]{1,0:T(8,128)(2,1)S(1)}, u32[]{:S(2)}, u32[]{:S(2)}) collective-permute-start(bf16[256,256]{1,0:T(8,128)(2,1)} %copy-done.7), channel_id=1, source_target_pairs={{0,192},{8,200},{16,208},{24,216},{32,224},{40,232},{48,240},{56,2... | collective-permute-start | bytes 393224 | tf_op jit(solution)/shard_map/ppermute | solution.py:19
  97.5 11.5 %collective-permute-start.20 = (bf16[128,768]{1,0:T(8,128)(2,1)S(1)}, bf16[128,768]{1,0:T(8,128)(2,1)S(1)}, u32[]{:S(2)}, u32[]{:S(2)}) collective-permute-start(bf16[128,768]{1,0:T(8,128)(2,1)S(1)} %get-tuple-element.56), channel_id=1, source_target_pairs={{0,64},{8,72},{16,80},{24,88},{32,96},{40,104},{48,112},{56,120},{... | collective-permute-start | bytes 589832 | tf_op jit(solution)/shard_map/ppermute | solution.py:19
  98.6 10.4 %collective-permute-start.21 = (bf16[128,768]{1,0:T(8,128)(2,1)S(1)}, bf16[128,768]{1,0:T(8,128)(2,1)S(1)}, u32[]{:S(2)}, u32[]{:S(2)}) collective-permute-start(bf16[128,768]{1,0:T(8,128)(2,1)S(1)} %get-tuple-element.57), channel_id=1, source_target_pairs={{0,192},{8,200},{16,208},{24,216},{32,224},{40,232},{48,240},{56,2... | collective-permute-start | bytes 589832 | tf_op jit(solution)/shard_map/ppermute | solution.py:19
  103.3 3.4 %collective-permute-start.22 = (bf16[128,256]{1,0:T(8,128)(2,1)S(1)}, bf16[128,256]{1,0:T(8,128)(2,1)S(1)}, u32[]{:S(2)}, u32[]{:S(2)}) collective-permute-start(bf16[128,256]{1,0:T(8,128)(2,1)S(1)} %get-tuple-element.58), channel_id=1, source_target_pairs={{0,16},{8,24},{16,0},{24,8},{32,48},{40,56},{48,32},{56,40},{64,80... | collective-permute-start | bytes 196616 | tf_op jit(solution)/shard_map/ppermute | solution.py:19
  109.1 11.4 %collective-permute-start.23 = (bf16[64,768]{1,0:T(8,128)(2,1)S(1)}, bf16[64,768]{1,0:T(8,128)(2,1)S(1)}, u32[]{:S(2)}, u32[]{:S(2)}) collective-permute-start(bf16[64,768]{1,0:T(8,128)(2,1)S(1)} %get-tuple-element.62), channel_id=1, source_target_pairs={{0,192},{8,200},{16,208},{24,216},{32,224},{40,232},{48,240},{56,2... | collective-permute-start | bytes 294920 | tf_op jit(solution)/shard_map/ppermute | solution.py:19
  111.2 9.3 %collective-permute-start.24 = (bf16[64,768]{1,0:T(8,128)(2,1)S(1)}, bf16[64,768]{1,0:T(8,128)(2,1)S(1)}, u32[]{:S(2)}, u32[]{:S(2)}) collective-permute-start(bf16[64,768]{1,0:T(8,128)(2,1)S(1)} %get-tuple-element.63), channel_id=1, source_target_pairs={{0,64},{8,72},{16,80},{24,88},{32,96},{40,104},{48,112},{56,120},{... | collective-permute-start | bytes 294920 | tf_op jit(solution)/shard_map/ppermute | solution.py:19
  116.3 4.3 %collective-permute-start.25 = (bf16[64,256]{1,0:T(8,128)(2,1)S(1)}, bf16[64,256]{1,0:T(8,128)(2,1)S(1)}, u32[]{:S(2)}, u32[]{:S(2)}) collective-permute-start(bf16[64,256]{1,0:T(8,128)(2,1)S(1)} %get-tuple-element.64), channel_id=1, source_target_pairs={{0,48},{8,56},{16,32},{24,40},{32,16},{40,24},{48,0},{56,8},{64,11... | collective-permute-start | bytes 98312 | tf_op jit(solution)/shard_map/ppermute | solution.py:19
  121.0 7.0 %collective-permute-start.28 = (bf16[64,768]{1,0:T(8,128)(2,1)S(1)}, bf16[64,768]{1,0:T(8,128)(2,1)S(1)}, u32[]{:S(2)}, u32[]{:S(2)}) collective-permute-start(bf16[64,768]{1,0:T(8,128)(2,1)S(1)} %get-tuple-element.67.refs_0_), channel_id=1, source_target_pairs={{0,192},{8,200},{16,208},{24,216},{32,224},{40,232},{48,240},{56,2... | collective-permute-start | bytes 294920 | tf_op jit(solution)/shard_map/ppermute | solution.py:19
  121.3 6.6 %collective-permute-start.29 = (bf16[64,768]{1,0:T(8,128)(2,1)S(1)}, bf16[64,768]{1,0:T(8,128)(2,1)S(1)}, u32[]{:S(2)}, u32[]{:S(2)}) collective-permute-start(bf16[64,768]{1,0:T(8,128)(2,1)S(1)} %get-tuple-element.68.refs_2_), channel_id=1, source_target_pairs={{0,64},{8,72},{16,80},{24,88},{32,96},{40,104},{48,112},{56,120},{... | collective-permute-start | bytes 294920 | tf_op jit(solution)/shard_map/ppermute | solution.py:19
  124.0 4.0 %collective-permute-start.30 = (bf16[64,256]{1,0:T(8,128)(2,1)S(1)}, bf16[64,256]{1,0:T(8,128)(2,1)S(1)}, u32[]{:S(2)}, u32[]{:S(2)}) collective-permute-start(bf16[64,256]{1,0:T(8,128)(2,1)S(1)} %get-tuple-element.69.refs_4_), channel_id=1, source_target_pairs={{0,48},{8,56},{16,32},{24,40},{32,16},{40,24},{48,0},{56,8},{64,11... | collective-permute-start | bytes 98312 | tf_op jit(solution)/shard_map/ppermute | solution.py:19
  128.0 7.7 %collective-permute-start.31 = (bf16[128,768]{1,0:T(8,128)(2,1)S(1)}, bf16[128,768]{1,0:T(8,128)(2,1)S(1)}, u32[]{:S(2)}, u32[]{:S(2)}) collective-permute-start(bf16[128,768]{1,0:T(8,128)(2,1)S(1)} %get-tuple-element.70.refs_0_), channel_id=1, source_target_pairs={{0,64},{8,72},{16,80},{24,88},{32,96},{40,104},{48,112},{56,120},{... | collective-permute-start | bytes 589832 | tf_op jit(solution)/shard_map/ppermute | solution.py:19
  128.6 7.7 %collective-permute-start.32 = (bf16[128,768]{1,0:T(8,128)(2,1)S(1)}, bf16[128,768]{1,0:T(8,128)(2,1)S(1)}, u32[]{:S(2)}, u32[]{:S(2)}) collective-permute-start(bf16[128,768]{1,0:T(8,128)(2,1)S(1)} %get-tuple-element.71.refs_2_), channel_id=1, source_target_pairs={{0,192},{8,200},{16,208},{24,216},{32,224},{40,232},{48,240},{56,2... | collective-permute-start | bytes 589832 | tf_op jit(solution)/shard_map/ppermute | solution.py:19
  131.6 3.1 %collective-permute-start.33 = (bf16[128,256]{1,0:T(8,128)(2,1)S(1)}, bf16[128,256]{1,0:T(8,128)(2,1)S(1)}, u32[]{:S(2)}, u32[]{:S(2)}) collective-permute-start(bf16[128,256]{1,0:T(8,128)(2,1)S(1)} %get-tuple-element.72.refs_4_), channel_id=1, source_target_pairs={{0,16},{8,24},{16,0},{24,8},{32,48},{40,56},{48,32},{56,40},{64,80... | collective-permute-start | bytes 196616 | tf_op jit(solution)/shard_map/ppermute | solution.py:19
  136.4 17.5 %collective-permute-start.34 = (bf16[256,768]{1,0:T(8,128)(2,1)S(1)}, bf16[256,768]{1,0:T(8,128)(2,1)S(1)}, u32[]{:S(2)}, u32[]{:S(2)}) collective-permute-start(bf16[256,768]{1,0:T(8,128)(2,1)S(1)} %get-tuple-element.73.refs_0_), channel_id=1, source_target_pairs={{0,48},{8,56},{16,32},{24,40},{32,16},{40,24},{48,0},{56,8},{64,11... | collective-permute-start | bytes 1179656 | tf_op jit(solution)/shard_map/ppermute | solution.py:19
  136.8 17.1 %collective-permute-start.35 = (bf16[256,768]{1,0:T(8,128)(2,1)S(1)}, bf16[256,768]{1,0:T(8,128)(2,1)S(1)}, u32[]{:S(2)}, u32[]{:S(2)}) collective-permute-start(bf16[256,768]{1,0:T(8,128)(2,1)S(1)} %get-tuple-element.74.refs_2_), channel_id=1, source_target_pairs={{0,16},{8,24},{16,0},{24,8},{32,48},{40,56},{48,32},{56,40},{64,80... | collective-permute-start | bytes 1179656 | tf_op jit(solution)/shard_map/ppermute | solution.py:19
  140.2 20.5 %collective-permute-start.27 = (f32[64,1792]{1,0:T(8,128)S(1)}, f32[64,1792]{1,0:T(8,128)S(1)}, u32[]{:S(2)}, u32[]{:S(2)}) collective-permute-start(f32[64,1792]{1,0:T(8,128)S(1)} %pad_maximum_fusion.1), channel_id=1, source_target_pairs={{0,8},{8,0},{16,24},{24,16},{32,40},{40,32},{48,56},{56,48},{64,72... | collective-permute-start | bytes 1376264 | tf_op jit(solution)/shard_map/ppermute | solution.py:19
  145.4 8.6 %collective-permute-start.36 = (bf16[256,256]{1,0:T(8,128)(2,1)S(1)}, bf16[256,256]{1,0:T(8,128)(2,1)S(1)}, u32[]{:S(2)}, u32[]{:S(2)}) collective-permute-start(bf16[256,256]{1,0:T(8,128)(2,1)S(1)} %get-tuple-element.75.refs_4_), channel_id=1, source_target_pairs={{0,192},{8,200},{16,208},{24,216},{32,224},{40,232},{48,240},{56,2... | collective-permute-start | bytes 393224 | tf_op jit(solution)/shard_map/ppermute | solution.py:19
  154.1 18.8 %collective-permute-start.37 = (bf16[512,768]{1,0:T(8,128)(2,1)S(1)}, bf16[512,768]{1,0:T(8,128)(2,1)S(1)}, u32[]{:S(2)}, u32[]{:S(2)}) collective-permute-start(bf16[512,768]{1,0:T(8,128)(2,1)S(1)} %get-tuple-element.76.refs_3_), channel_id=1, source_target_pairs={{0,16},{8,24},{16,0},{24,8},{32,48},{40,56},{48,32},{56,40},{64,80... | collective-permute-start | bytes 2359304 | tf_op jit(solution)/shard_map/ppermute | solution.py:19
  155.9 19.5 %collective-permute-start.38 = (bf16[512,768]{1,0:T(8,128)(2,1)S(1)}, bf16[512,768]{1,0:T(8,128)(2,1)S(1)}, u32[]{:S(2)}, u32[]{:S(2)}) collective-permute-start(bf16[512,768]{1,0:T(8,128)(2,1)S(1)} %get-tuple-element.77.refs_4_), channel_id=1, source_target_pairs={{0,48},{8,56},{16,32},{24,40},{32,16},{40,24},{48,0},{56,8},{64,11... | collective-permute-start | bytes 2359304 | tf_op jit(solution)/shard_map/ppermute | solution.py:19
  157.1 15.8 %collective-permute-start.39 = (bf16[512,256]{1,0:T(8,128)(2,1)S(1)}, bf16[512,256]{1,0:T(8,128)(2,1)S(1)}, u32[]{:S(2)}, u32[]{:S(2)}) collective-permute-start(bf16[512,256]{1,0:T(8,128)(2,1)S(1)} %get-tuple-element.78.refs_5_), channel_id=1, source_target_pairs={{0,64},{8,72},{16,80},{24,88},{32,96},{40,104},{48,112},{56,120},{... | collective-permute-start | bytes 786440 | tf_op jit(solution)/shard_map/ppermute | solution.py:19
  176.1 4.0 %collective-permute-start.40 = (bf16[256,1792]{1,0:T(8,128)(2,1)S(1)}, bf16[256,1792]{1,0:T(8,128)(2,1)S(1)}, u32[]{:S(2)}, u32[]{:S(2)}) collective-permute-start(bf16[256,1792]{1,0:T(8,128)(2,1)S(1)} %shard_map.164), channel_id=1, source_target_pairs={{0,8},{8,0},{16,24},{24,16},{32,40},{40,32},{48,56},{56,48},{64,72... | collective-permute-start | bytes 2752520 | tf_op jit(solution)/shard_map/ppermute | solution.py:19
  (10 other events, 12.3 us)
where the time goes:
time: 182 us
  starting transfers between devices  74.2 us (41%)
  waiting for transfers between devices  67.3 us (37%)
  local copies, waits for them, and re-layouts  18.4 us (10%)
  Pallas kernels  10 us (5%)
  matrix products  5.61 us (3%)
  other arithmetic  5.05 us (3%)
    ppermute x41, starting transfers between devices, swap(): return lax.ppermute(array, axis, [(i, i ^ mask) for i in range(count)])  74.2 us
    ppermute x41, waiting for transfers between devices, swap(): return lax.ppermute(array, axis, [(i, i ^ mask) for i in range(count)])  67.3 us
    pallas_call x17, Pallas kernels, call(): pl.pallas_call(body, out_shape=list(outs), in_specs=specs, out_specs=[pl....  10 us
    unnamed x36, local copies, waits for them, and re-layouts  8.64 us
    dot_general x3, matrix products, body(): factors.append(jnp.dot(both, choose, preferred_element_type=F32).astype(BF))  3.95 us
  transfers between devices with their start and end apart: 41, of which 22 were waited for; matrix products, arithmetic and copies ran while one was open for 10% of the time, Pallas kernels for 5%

commit v1 on v0

--- a/solution.py
+++ b/solution.py
@@ -14,9 +14,17 @@
 MIB = 2**20
 
 
-def swap(array, axis, mask):
-    count = lax.axis_size(axis)
-    return lax.ppermute(array, axis, [(i, i ^ mask) for i in range(count)])
+def swap(array, axis, masks):
+    inner = lax.axis_size("tp")
+    count = lax.axis_size("fsdp") * inner
+    scale = inner if axis == "fsdp" else 1
+    return lax.ppermute(
+        array, ("fsdp", "tp"), [(i, i ^ (scale * masks[i // inner % 2])) for i in range(count)]
+    )
+
+
+def swap_core(array):
+    return swap(array, "fsdp", (1, 1))
 
 
 def doubled(masks):
@@ -26,8 +34,9 @@
     return order
 
 
-def table(order):
-    return jnp.array(order, dtype=jnp.int32)
+def table(core, orders):
+    first, second = (jnp.array(order, dtype=jnp.int32) for order in orders)
+    return jnp.where(core == 0, first, second)
 
 
 def by_core(core, own, other, axis):
@@ -38,7 +47,7 @@
     )
 
 
-def call(kernel, outs, args, flops=0, vmem=16, scratch=(), smem=0, after=()):
+def call(kernel, outs, args, flops=0, vmem=8, scratch=(), smem=0, after=()):
     moved = sum(a.size * a.dtype.itemsize for a in args)
     moved += sum(o.size * o.dtype.itemsize for o in outs)
     specs = [
@@ -95,7 +104,7 @@
 def reorder(array, index, width):
     outs = [shape(array.shape[0], array.shape[1], array.dtype)]
     return call(
-        functools.partial(reorder_kernel, width), outs, [index, array], vmem=24, smem=1
+        functools.partial(reorder_kernel, width), outs, [index, array], vmem=8, smem=1
     )[0]
 
 
@@ -106,9 +115,11 @@
     for part, out_ref in enumerate(outs):
         blocks = out_ref.shape[0] // block
         for k in range(blocks):
-            start = pl.multiple_of(index_ref[part * blocks + k] * block, block)
-            chosen[k * block : (k + 1) * block, :tokens] = own_ref[pl.ds(start, block), :]
-            chosen[k * block : (k + 1) * block, tokens:] = other_ref[pl.ds(start, block), :]
+            row = slice(k * block, (k + 1) * block)
+            start = pl.multiple_of(index_ref[0, part * blocks + k] * block, block)
+            chosen[row, :tokens] = own_ref[pl.ds(start, block), :]
+            start = pl.multiple_of(index_ref[1, part * blocks + k] * block, block)
+            chosen[row, tokens:] = other_ref[pl.ds(start, block), :]
         width = out_ref.shape[1]
         out_ref[...] = jnp.dot(
             chosen[...], grads_ref[:, at : at + width], preferred_element_type=F32
@@ -122,7 +133,7 @@
         [shape(rows, w, kind) for w in widths],
         [index, own, other, grads],
         flops=2 * rows * grads.size,
-        vmem=24,
+        vmem=12,
         scratch=[pltpu.VMEM((rows, 2 * own.shape[1]), BF)],
         smem=1,
         after=after,
@@ -210,8 +221,8 @@
     rank = projector.shape[1]
     block = rank // 16
     column_count = rank // 8
-    wide = half * 3 // 7
-    widths = (wide, wide, half - 2 * wide)
+    wide = half * 5 // 7
+    widths = (wide, half - wide)
     rows = first_moment.shape[0]
 
     def my_half(array):
@@ -221,11 +232,14 @@
         return lax.dynamic_slice_in_dim(array, (1 - core) * half, half, 1)
 
     columns = lax.dynamic_slice_in_dim(projector, tp_place * column_count, column_count, 1)
-    columns = stack([[columns] + [swap(columns, "fsdp", m) for m in (8, 16, 24)]])[0]
-    columns = stack([[columns] + [swap(columns, "fsdp", m) for m in (2, 4, 6)]])[0]
-    columns_other = swap(columns, "fsdp", 1)
-    order = [x + z for x in (0, 2, 4, 6) for z in (0, 8, 16, 24)]
-    index = jnp.concatenate([place ^ c ^ table(order) for c in range(2)])
+    column_orders = ([8, 24, 2, 6], [24, 8, 6, 2])
+    for masks in zip(*column_orders):
+        columns = stack([[columns, swap(columns, "fsdp", masks)]])[0]
+    columns_other = swap_core(columns)
+    order = [doubled(o) for o in column_orders]
+    index = jnp.concatenate(
+        [place ^ table(core, order), place ^ 1 ^ table(1 - core, order)]
+    )
     act = reorder(activations, index, projector.shape[0])
     depth = columns.shape[0]
     dims = (((0,), (1,)), ((), ()))
@@ -233,57 +247,68 @@
     own = own + lax.dot_general(columns_other, act[:, depth:], dims, preferred_element_type=F32)
     own = own.astype(BF)
 
-    coords = stack([[own, swap(own, "tp", 1)]])[0]
-    coords = stack([[coords] + [swap(coords, "tp", m) for m in (2, 4, 6)]])[0]
-    coords_other = swap(coords, "fsdp", 1)
+    coords = own
+    for masks in ((1, 1), (2, 6), (6, 2)):
+        coords = stack([[coords, swap(coords, "tp", masks)]])[0]
+    coords_other = swap_core(coords)
+
+    def position(wanted, which):
+        part = tp_place ^ (wanted >> 1)
+        high = part >> 2
+        mixed = ((part >> 1) ^ high) & 1
+        upper = jnp.where(which == 0, 2 * mixed + 4 * high, 2 * high + 4 * mixed)
+        return 2 * ((part & 1) + upper) + (wanted & 1)
 
     grads = jnp.concatenate(
-        [my_half(grad_output), swap(other_half(grad_output), "fsdp", 1)], axis=0
+        [my_half(grad_output), swap_core(other_half(grad_output))], axis=0
     )
     moments = jnp.concatenate([first_moment, second_moment], axis=0)
-    moments_other = swap(other_half(moments), "fsdp", 1)
+    moments_other = swap_core(other_half(moments))
     moments_own = my_half(moments)
     first = by_core(core, moments_own[:rows], moments_other[:rows], 0)
     second = by_core(core, moments_own[rows:], moments_other[rows:], 0)
-    both = jnp.concatenate([projector, swap(projector, "fsdp", 1)], axis=0)
-
-    sum_orders = ([1, 3, 4, 12], [3, 1, 12, 4], [4, 12, 1, 3])
+    both = jnp.concatenate([projector, swap_core(projector)], axis=0)
+
+    sum_orders = (([1, 3, 4, 12], [3, 1, 12, 4]), ([4, 12, 1, 3], [12, 4, 3, 1]))
+    back_orders = [[o[::-1] for o in orders] for orders in sum_orders]
     keep_index, send_index = [], []
-    for masks in sum_orders:
-        wanted = chip ^ table(doubled(masks[::-1]))
-        position = 2 * (tp_place ^ (wanted >> 1)) + (wanted & 1)
-        keep_index.append(position[:8])
-        send_index.append(position[8:])
-    back_orders = [m[::-1] for m in sum_orders]
+    for orders in sum_orders:
+        wanted = chip ^ table(core, [doubled(o[::-1]) for o in orders])
+        places = jnp.stack([position(wanted, core), position(wanted, 1 - core)])
+        keep_index.append(places[:, :8])
+        send_index.append(places[:, 8:])
     ranks = jnp.arange(rank, dtype=jnp.int32)
     factors = []
-    for masks in back_orders:
-        blocks = chip ^ table(doubled(masks))
+    for orders in back_orders:
+        blocks = chip ^ table(core, [doubled(o) for o in orders])
         wanted = (blocks[:, None] * block + ranks[None, :block]).reshape(-1)
         choose = (ranks[:, None] == wanted[None, :]).astype(BF)
         factors.append(jnp.dot(both, choose, preferred_element_type=F32).astype(BF))
+
+    def exchange(arrays, orders_of, stage):
+        return [
+            swap(a, "fsdp", [2 * o[stage] for o in orders]) for a, orders in zip(arrays, orders_of)
+        ]
+
     arrays = (coords, coords_other, grads, rank // 2, widths, block)
-    sent = partial_sums(jnp.concatenate(send_index), *arrays, BF)
-    kept = partial_sums(jnp.concatenate(keep_index), *arrays, F32, after=factors)
+    sent = partial_sums(jnp.concatenate(send_index, axis=1), *arrays, BF)
+    kept = partial_sums(jnp.concatenate(keep_index, axis=1), *arrays, F32, after=factors)
     for stage in range(3):
-        got = [swap(s, "fsdp", 2 * m[stage]) for s, m in zip(sent, sum_orders)]
-        kept, sent = halve(kept, got)
-    got = [swap(s, "fsdp", 2 * m[3]) for s, m in zip(sent, sum_orders)]
+        kept, sent = halve(kept, exchange(sent, sum_orders, stage))
+    got = exchange(sent, sum_orders, 3)
     new_first, new_second, parts = adam(kept, got, first, second)
 
     def rows_of(array, which):
         return lax.dynamic_slice_in_dim(array, which * rows, rows, 0)
 
-    states_other = swap(
-        jnp.concatenate([rows_of(new_first, 1 - core), rows_of(new_second, 1 - core)], axis=0),
-        "fsdp",
-        1,
+    states_other = swap_core(
+        jnp.concatenate([rows_of(new_first, 1 - core), rows_of(new_second, 1 - core)], axis=0)
     )
     out_first = by_core(core, rows_of(new_first, core), states_other[:rows], 1)
     out_second = by_core(core, rows_of(new_second, core), states_other[rows:], 1)
 
     for stage in range(4):
-        got = [swap(p, "fsdp", 2 * m[stage]) for p, m in zip(parts, back_orders)]
+        got = exchange(parts, back_orders, stage)
         if stage < 3:
             parts = stack([[p, g] for p, g in zip(parts, got)])
     count = len(parts)
@@ -293,7 +318,7 @@
         [shape(both.shape[0], half, F32)],
         [*factors, *parts],
         flops=flops,
-        vmem=32,
+        vmem=12,
     )[0]
     late = [
         call(
@@ -301,11 +326,11 @@
             [shape(tokens, half, BF)],
             [*factors, *got, early],
             flops=flops // 2,
-            vmem=32,
+            vmem=12,
         )[0]
         for row in (tokens, 0)
     ]
-    update = by_core(core, late[1], swap(late[0], "fsdp", 1), 1)
+    update = by_core(core, late[1], swap_core(late[0]), 1)
     return (out_first, out_second, update)
 
 

time: 182 us -> 201 us (1.10)
  starting transfers between devices: 74.2 us -> 82 us
  waiting for transfers between devices: 67.3 us -> 73.8 us
  Pallas kernels: 10 us -> 14.4 us
  local copies, waits for them, and re-layouts: 18.4 us -> 16.2 us
    ppermute x41 -> x30, starting transfers between devices: 74.2 us -> 82 us  [swap(): lax.ppermute(array, ('fsdp', 'tp'), [(i, i ^ scale * masks[i // inner % 2...]
    ppermute x41 -> x30, waiting for transfers between devices: 67.3 us -> 73.8 us  [swap(): lax.ppermute(array, ('fsdp', 'tp'), [(i, i ^ scale * masks[i // inner % 2...]
    pallas_call x17 -> x20, Pallas kernels: 10 us -> 14.4 us  [call(): pl.pallas_call(body, out_shape=list(outs), in_specs=specs, out_specs=[pl....]
    concatenate x1, local copies, waits for them, and re-layouts: 0.04 us -> 2.21 us  [body(): both = jnp.concatenate([projector, swap_core(projector)], axis=0)]
    unnamed x36 -> x46, local copies, waits for them, and re-layouts: 8.64 us -> 7.13 us
  transfers between devices with their start and end apart: 41 -> 30, of which waited for: 22 -> 20; matrix products, arithmetic and copies ran while one was open for 10% -> 10% of each run, Pallas kernels for 5% -> 4%
where the time goes in v1:
time: 201 us; the launch traced here: 199 us
  starting transfers between devices  82 us (41%)
  waiting for transfers between devices  73.8 us (37%)
  local copies, waits for them, and re-layouts  16.2 us (8%)
  Pallas kernels  14.4 us (7%)
  matrix products  6.78 us (3%)
  other arithmetic  4.99 us (2%)
    ppermute x30, starting transfers between devices, swap(): lax.ppermute(array, ('fsdp', 'tp'), [(i, i ^ scale * masks[i // inner % 2...  82 us
    ppermute x30, waiting for transfers between devices, swap(): lax.ppermute(array, ('fsdp', 'tp'), [(i, i ^ scale * masks[i // inner % 2...  73.8 us
    pallas_call x20, Pallas kernels, call(): pl.pallas_call(body, out_shape=list(outs), in_specs=specs, out_specs=[pl....  14.4 us
    unnamed x46, local copies, waits for them, and re-layouts  7.13 us
  transfers between devices with their start and end apart: 30, of which 20 were waited for; matrix products, arithmetic and copies ran while one was open for 10% of the time, Pallas kernels for 4%

profile of v1, /device:TPU:1, one launch (start us, length us, event | category | flops | bytes accessed | tf_op | source)
XLA Modules:
  0.0 199.1 jit_solution(17863134349806058088)
XLA Ops:
  1.6 6.8 %collective-permute-start = (bf16[256,128]{1,0:T(8,128)(2,1)S(1)}, bf16[256,128]{1,0:T(8,128)(2,1)S(1)}, u32[]{:S(2)}, u32[]{:S(2)}) collective-permute-start(bf16[256,128]{1,0:T(8,128)(2,1)S(1)} %constant_dynamic-slice_fusion.8.refs_0_), channel_id=1, source_target_pairs={{0,64},{1,65},{2,66},{3,67},{4,68},{5,69},{6,70},{7,71},{8,200},{9... | collective-permute-start | bytes 196616 | tf_op jit(solution)/shard_map/ppermute | solution.py:21
  8.5 1.8 collective-permute-done.refs_1_
  11.4 5.3 %collective-permute-done.1.refs_1_ = bf16[512,128]{1,0:T(8,128)(2,1)S(1)} collective-permute-done((bf16[512,128]{1,0:T(8,128)(2,1)S(1)}, bf16[512,128]{1,0:T(8,128)(2,1)S(1)}, u32[]{:S(2)}, u32[]{:S(2)}) %collective-permute-start.1) | collective-permute-done | bytes 131104 | tf_op jit(solution)/shard_map/ppermute | solution.py:21
  16.8 2.6 %collective-permute-start.2 = (bf16[1024,128]{1,0:T(8,128)(2,1)S(1)}, bf16[1024,128]{1,0:T(8,128)(2,1)S(1)}, u32[]{:S(2)}, u32[]{:S(2)}) collective-permute-start(bf16[1024,128]{1,0:T(8,128)(2,1)S(1)} %shard_map.185.refs_0_), channel_id=1, source_target_pairs={{0,16},{1,17},{2,18},{3,19},{4,20},{5,21},{6,22},{7,23},{8,56},{9,... | collective-permute-start | bytes 786440 | tf_op jit(solution)/shard_map/ppermute | solution.py:21
  19.3 4.0 %collective-permute-done.2.refs_1_ = bf16[1024,128]{1,0:T(8,128)(2,1)S(1)} collective-permute-done((bf16[1024,128]{1,0:T(8,128)(2,1)S(1)}, bf16[1024,128]{1,0:T(8,128)(2,1)S(1)}, u32[]{:S(2)}, u32[]{:S(2)}) %collective-permute-start.2) | collective-permute-done | bytes 262176 | tf_op jit(solution)/shard_map/ppermute | solution.py:21
  23.4 5.4 %collective-permute-start.10 = (bf16[256,1024]{1,0:T(8,128)(2,1)}, bf16[256,1024]{1,0:T(8,128)(2,1)}, u32[]{:S(2)}, u32[]{:S(2)}) collective-permute-start(bf16[256,1024]{1,0:T(8,128)(2,1)} %param.19), channel_id=1, source_target_pairs={{0,8},{1,9},{2,10},{3,11},{4,12},{5,13},{6,14},{7,15},{8,0},{9,1},... | collective-permute-start | bytes 1572872 | tf_op jit(solution)/shard_map/ppermute | solution.py:21
  28.8 1.4 constant_dynamic-slice_fusion.7
  30.2 1.5 collective-permute-done.3.refs_1_
  31.8 4.8 %collective-permute-start.4 = (bf16[4096,128]{1,0:T(8,128)(2,1)S(1)}, bf16[4096,128]{1,0:T(8,128)(2,1)}, u32[]{:S(2)}, u32[]{:S(2)}) collective-permute-start(bf16[4096,128]{1,0:T(8,128)(2,1)S(1)} %shard_map.187), channel_id=1, source_target_pairs={{0,8},{1,9},{2,10},{3,11},{4,12},{5,13},{6,14},{7,15},{8,0},{9,1},... | collective-permute-start | bytes 3145736 | tf_op jit(solution)/shard_map/ppermute | solution.py:21
  36.7 2.2 %copy-done.2 = bf16[256,8192]{1,0:T(8,128)(2,1)S(1)} copy-done((bf16[256,8192]{1,0:T(8,128)(2,1)S(1)}, bf16[256,8192]{1,0:T(8,128)(2,1)}, u32[]{:S(2)}) %copy-start.2) | copy-done | bytes 4194328
  40.2 2.1 %fusion.2 = f32[128,256]{1,0:T(8,128)S(1)} fusion(bf16[4096,128]{1,0:T(8,128)(2,1)} %collective-permute-done.4, bf16[256,8192]{1,0:T(8,128)(2,1)S(1)} %shard_map.188), kind=kOutput, calls=%fused_computation.4 | convolution fusion | flops 268435456 | bytes 3276800 | tf_op jit(solution)/shard_map/dot_general | solution.py:247
  43.3 3.6 %collective-permute-done.5.refs_1_ = bf16[128,256]{1,0:T(8,128)(2,1)S(1)} collective-permute-done((bf16[128,256]{1,0:T(8,128)(2,1)S(1)}, bf16[128,256]{1,0:T(8,128)(2,1)S(1)}, u32[]{:S(2)}, u32[]{:S(2)}) %collective-permute-start.5) | collective-permute-done | bytes 65568 | tf_op jit(solution)/shard_map/ppermute | solution.py:21
  46.9 2.8 %collective-permute-start.6 = (bf16[256,256]{1,0:T(8,128)(2,1)S(1)}, bf16[256,256]{1,0:T(8,128)(2,1)S(1)}, u32[]{:S(2)}, u32[]{:S(2)}) collective-permute-start(bf16[256,256]{1,0:T(8,128)(2,1)S(1)} %shard_map.189.refs_0_), channel_id=1, source_target_pairs={{0,2},{1,3},{2,0},{3,1},{4,6},{5,7},{6,4},{7,5},{8,14},{9,15},{10,... | collective-permute-start | bytes 393224 | tf_op jit(solution)/shard_map/ppermute | solution.py:21
  49.8 2.3 %collective-permute-done.6.refs_1_ = bf16[256,256]{1,0:T(8,128)(2,1)S(1)} collective-permute-done((bf16[256,256]{1,0:T(8,128)(2,1)S(1)}, bf16[256,256]{1,0:T(8,128)(2,1)S(1)}, u32[]{:S(2)}, u32[]{:S(2)}) %collective-permute-start.6) | collective-permute-done | bytes 131104 | tf_op jit(solution)/shard_map/ppermute | solution.py:21
  53.4 4.3 %collective-permute-done.7.refs_1_ = bf16[512,256]{1,0:T(8,128)(2,1)S(1)} collective-permute-done((bf16[512,256]{1,0:T(8,128)(2,1)S(1)}, bf16[512,256]{1,0:T(8,128)(2,1)S(1)}, u32[]{:S(2)}, u32[]{:S(2)}) %collective-permute-start.7) | collective-permute-done | bytes 262176 | tf_op jit(solution)/shard_map/ppermute | solution.py:21
  57.8 2.9 %collective-permute-start.8 = (bf16[1024,256]{1,0:T(8,128)(2,1)S(1)}, bf16[1024,256]{1,0:T(8,128)(2,1)S(1)}, u32[]{:S(2)}, u32[]{:S(2)}) collective-permute-start(bf16[1024,256]{1,0:T(8,128)(2,1)S(1)} %shard_map.191.refs_1_), channel_id=1, source_target_pairs={{0,8},{1,9},{2,10},{3,11},{4,12},{5,13},{6,14},{7,15},{8,0},{9,1},... | collective-permute-start | bytes 1572872 | tf_op jit(solution)/shard_map/ppermute | solution.py:21
  60.8 1.3 pad_maximum_fusion.refs_3_
  62.2 2.7 %shard_map.193 = (bf16[512,1280]{1,0:T(8,128)(2,1)}, bf16[512,512]{1,0:T(8,128)(2,1)}) custom-call(s32[2,16]{1,0:T(2,128)S(1)} %pad_add_fusion.3.refs_0_, bf16[1024,256]{1,0:T(8,128)(2,1)S(1)} %shard_map.191.refs_1_, bf16[1024,256]{1,0:T(8,128)(2,1)S(1)} %collective-permute-done.8.refs_2_, bf16[512,1792]{1,0:T(8,128)(2,1)S(1)} %pad_maximum_fusion.refs_3_), custom_call_target="tpu_custom_call" | custom-call | flops 939524096 | bytes 4718720 | tf_op jit(solution)/shard_map/pallas_call | solution.py:63
  66.1 2.5 %collective-permute-start.11 = (bf16[512,1280]{1,0:T(8,128)(2,1)}, bf16[512,1280]{1,0:T(8,128)(2,1)}, u32[]{:S(2)}, u32[]{:S(2)}) collective-permute-start(bf16[512,1280]{1,0:T(8,128)(2,1)} %get-tuple-element.31), channel_id=1, source_target_pairs={{0,16},{1,17},{2,18},{3,19},{4,20},{5,21},{6,22},{7,23},{8,56},{9,... | collective-permute-start | bytes 3932168 | tf_op jit(solution)/shard_map/ppermute | solution.py:21
  68.9 2.2 %constant_dynamic-update-slice_fusion = bf16[512,1024]{1,0:T(8,128)(2,1)} fusion(bf16[512,1024]{1,0:T(8,128)(2,1)} %constant_dynamic-update-slice_fusion.1, bf16[256,1024]{1,0:T(8,128)(2,1)} %collective-permute-done.10), kind=kLoop, calls=%fused_computation.21 | loop fusion | bytes 1048576 | tf_op jit(solution)/shard_map/concatenate | solution.py:270
  71.1 5.1 %collective-permute-start.12 = (bf16[512,512]{1,0:T(8,128)(2,1)}, bf16[512,512]{1,0:T(8,128)(2,1)S(1)}, u32[]{:S(2)}, u32[]{:S(2)}) collective-permute-start(bf16[512,512]{1,0:T(8,128)(2,1)} %get-tuple-element.32), channel_id=1, source_target_pairs={{0,64},{1,65},{2,66},{3,67},{4,68},{5,69},{6,70},{7,71},{8,200},{9... | collective-permute-start | bytes 1572872 | tf_op jit(solution)/shard_map/ppermute | solution.py:21
  76.2 2.5 %fusion.8.refs_5_.refs_1_ = bf16[512,1024]{1,0:T(8,128)(2,1)S(1)} fusion(bf16[512,1024]{1,0:T(8,128)(2,1)} %constant_dynamic-update-slice_fusion, s32[1024]{0:T(1024)S(1)} %add.124), kind=kOutput, calls=%fused_computation.12 | convolution fusion | flops 1075314688 | bytes 2101248 | tf_op jit(solution)/shard_map/dot_general | solution.py:286
  78.7 1.3 fusion.9.refs_4_.refs_0_
  80.2 1.7 shard_map.192
  81.9 4.8 %collective-permute-done.12.refs_3_ = bf16[512,512]{1,0:T(8,128)(2,1)S(1)} collective-permute-done((bf16[512,512]{1,0:T(8,128)(2,1)}, bf16[512,512]{1,0:T(8,128)(2,1)S(1)}, u32[]{:S(2)}, u32[]{:S(2)}) %collective-permute-start.12) | collective-permute-done | bytes 524320 | tf_op jit(solution)/shard_map/ppermute | solution.py:21
  86.7 2.6 %shard_map.194 = (f32[256,1280]{1,0:T(8,128)S(1)}, f32[256,512]{1,0:T(8,128)S(1)}, bf16[256,1280]{1,0:T(8,128)(2,1)}, bf16[256,512]{1,0:T(8,128)(2,1)}) custom-call(f32[512,1280]{1,0:T(8,128)S(1)} %get-tuple-element.29.refs_0_, f32[512,512]{1,0:T(8,128)S(1)} %get-tuple-element.30.refs_1_, bf16[512,1280]{1,0:T(8,128)(2,1)} %collective-permute-done.11.refs_2_, ...), custom_call_target="tpu_custom_call" | custom-call | bytes 8257536 | tf_op jit(solution)/shard_map/pallas_call | solution.py:63
  92.0 2.5 %collective-permute-start.14 = (bf16[256,512]{1,0:T(8,128)(2,1)}, bf16[256,512]{1,0:T(8,128)(2,1)}, u32[]{:S(2)}, u32[]{:S(2)}) collective-permute-start(bf16[256,512]{1,0:T(8,128)(2,1)} %get-tuple-element.36), channel_id=1, source_target_pairs={{0,192},{1,193},{2,194},{3,195},{4,196},{5,197},{6,198},{7,199},{8... | collective-permute-start | bytes 786440 | tf_op jit(solution)/shard_map/ppermute | solution.py:21
  95.6 6.1 %collective-permute-done.14.refs_3_ = bf16[256,512]{1,0:T(8,128)(2,1)} collective-permute-done((bf16[256,512]{1,0:T(8,128)(2,1)}, bf16[256,512]{1,0:T(8,128)(2,1)}, u32[]{:S(2)}, u32[]{:S(2)}) %collective-permute-start.14) | collective-permute-done | bytes 262176 | tf_op jit(solution)/shard_map/ppermute | solution.py:21
  102.8 1.3 shard_map.195
  104.1 3.7 %collective-permute-start.15 = (bf16[128,1280]{1,0:T(8,128)(2,1)S(1)}, bf16[128,1280]{1,0:T(8,128)(2,1)S(1)}, u32[]{:S(2)}, u32[]{:S(2)}) collective-permute-start(bf16[128,1280]{1,0:T(8,128)(2,1)S(1)} %get-tuple-element.39), channel_id=1, source_target_pairs={{0,64},{1,65},{2,66},{3,67},{4,68},{5,69},{6,70},{7,71},{8,200},{9... | collective-permute-start | bytes 983048 | tf_op jit(solution)/shard_map/ppermute | solution.py:21
  109.4 3.6 %collective-permute-done.16.refs_3_ = bf16[128,512]{1,0:T(8,128)(2,1)S(1)} collective-permute-done((bf16[128,512]{1,0:T(8,128)(2,1)S(1)}, bf16[128,512]{1,0:T(8,128)(2,1)S(1)}, u32[]{:S(2)}, u32[]{:S(2)}) %collective-permute-start.16) | collective-permute-done | bytes 131104 | tf_op jit(solution)/shard_map/ppermute | solution.py:21
  113.0 1.3 collective-permute-done.15.refs_2_
  114.3 1.3 collective-permute-start.17
  115.7 1.4 collective-permute-start.18
  117.1 1.6 collective-permute-done.18.refs_3_
  121.9 1.5 collective-permute-start.22
  123.4 1.9 collective-permute-done.22.refs_3_
  126.1 5.7 %collective-permute-start.23 = (bf16[128,1280]{1,0:T(8,128)(2,1)S(1)}, bf16[128,1280]{1,0:T(8,128)(2,1)S(1)}, u32[]{:S(2)}, u32[]{:S(2)}) collective-permute-start(bf16[128,1280]{1,0:T(8,128)(2,1)S(1)} %get-tuple-element.49.refs_0_), channel_id=1, source_target_pairs={{0,64},{1,65},{2,66},{3,67},{4,68},{5,69},{6,70},{7,71},{8,200},{9... | collective-permute-start | bytes 983048 | tf_op jit(solution)/shard_map/ppermute | solution.py:21
  132.3 5.5 %collective-permute-done.24.refs_3_ = bf16[128,512]{1,0:T(8,128)(2,1)S(1)} collective-permute-done((bf16[128,512]{1,0:T(8,128)(2,1)S(1)}, bf16[128,512]{1,0:T(8,128)(2,1)S(1)}, u32[]{:S(2)}, u32[]{:S(2)}) %collective-permute-start.24) | collective-permute-done | bytes 131104 | tf_op jit(solution)/shard_map/ppermute | solution.py:21
  137.7 3.0 %collective-permute-done.23.refs_1_ = bf16[128,1280]{1,0:T(8,128)(2,1)S(1)} collective-permute-done((bf16[128,1280]{1,0:T(8,128)(2,1)S(1)}, bf16[128,1280]{1,0:T(8,128)(2,1)S(1)}, u32[]{:S(2)}, u32[]{:S(2)}) %collective-permute-start.23) | collective-permute-done | bytes 327712 | tf_op jit(solution)/shard_map/ppermute | solution.py:21
  141.5 3.1 %collective-permute-start.26 = (bf16[256,512]{1,0:T(8,128)(2,1)}, bf16[256,512]{1,0:T(8,128)(2,1)}, u32[]{:S(2)}, u32[]{:S(2)}) collective-permute-start(bf16[256,512]{1,0:T(8,128)(2,1)} %get-tuple-element.52.refs_2_), channel_id=1, source_target_pairs={{0,192},{1,193},{2,194},{3,195},{4,196},{5,197},{6,198},{7,199},{8... | collective-permute-start | bytes 786440 | tf_op jit(solution)/shard_map/ppermute | solution.py:21
  145.8 9.1 %collective-permute-done.26.refs_3_ = bf16[256,512]{1,0:T(8,128)(2,1)} collective-permute-done((bf16[256,512]{1,0:T(8,128)(2,1)}, bf16[256,512]{1,0:T(8,128)(2,1)}, u32[]{:S(2)}, u32[]{:S(2)}) %collective-permute-start.26) | collective-permute-done | bytes 262176 | tf_op jit(solution)/shard_map/ppermute | solution.py:21
  156.1 3.2 %collective-permute-start.27 = (bf16[512,1280]{1,0:T(8,128)(2,1)S(1)}, bf16[512,1280]{1,0:T(8,128)(2,1)S(1)}, u32[]{:S(2)}, u32[]{:S(2)}) collective-permute-start(bf16[512,1280]{1,0:T(8,128)(2,1)S(1)} %get-tuple-element.53.refs_2_), channel_id=1, source_target_pairs={{0,16},{1,17},{2,18},{3,19},{4,20},{5,21},{6,22},{7,23},{8,56},{9,... | collective-permute-start | bytes 3932168 | tf_op jit(solution)/shard_map/ppermute | solution.py:21
  159.3 17.8 %collective-permute-start.20 = (f32[64,1792]{1,0:T(8,128)S(1)}, f32[64,1792]{1,0:T(8,128)S(1)}, u32[]{:S(2)}, u32[]{:S(2)}) collective-permute-start(f32[64,1792]{1,0:T(8,128)S(1)} %pad_maximum_fusion.1), channel_id=1, source_target_pairs={{0,8},{1,9},{2,10},{3,11},{4,12},{5,13},{6,14},{7,15},{8,0},{9,1},... | collective-permute-start | bytes 1376264 | tf_op jit(solution)/shard_map/ppermute | solution.py:21
  177.1 2.0 collective-permute-start.28
  180.2 12.5 %collective-permute-done.28.refs_3_ = bf16[512,512]{1,0:T(8,128)(2,1)S(1)} collective-permute-done((bf16[512,512]{1,0:T(8,128)(2,1)S(1)}, bf16[512,512]{1,0:T(8,128)(2,1)S(1)}, u32[]{:S(2)}, u32[]{:S(2)}) %collective-permute-start.28) | collective-permute-done | bytes 524320 | tf_op jit(solution)/shard_map/ppermute | solution.py:21
  193.4 1.9 collective-permute-start.29
  197.5 1.6 maximum_select_fusion
  (112 shorter events, 26.0 us)
Async XLA Ops:
  0.6 28.2 %copy-start.11 = (bf16[256,3584]{1,0:T(8,128)(2,1)S(1)}, bf16[256,3584]{1,0:T(8,128)(2,1)}, u32[]{:S(2)}) copy-start(bf16[256,3584]{1,0:T(8,128)(2,1)} %param.18) | copy-start | bytes 5505028
  1.6 8.6 %collective-permute-start = (bf16[256,128]{1,0:T(8,128)(2,1)S(1)}, bf16[256,128]{1,0:T(8,128)(2,1)S(1)}, u32[]{:S(2)}, u32[]{:S(2)}) collective-permute-start(bf16[256,128]{1,0:T(8,128)(2,1)S(1)} %constant_dynamic-slice_fusion.8.refs_0_), channel_id=1, source_target_pairs={{0,64},{1,65},{2,66},{3,67},{4,68},{5,69},{6,70},{7,71},{8,200},{9... | collective-permute-start | bytes 196616 | tf_op jit(solution)/shard_map/ppermute | solution.py:21
  10.2 6.5 %collective-permute-start.1 = (bf16[512,128]{1,0:T(8,128)(2,1)S(1)}, bf16[512,128]{1,0:T(8,128)(2,1)S(1)}, u32[]{:S(2)}, u32[]{:S(2)}) collective-permute-start(bf16[512,128]{1,0:T(8,128)(2,1)S(1)} %shard_map.184.refs_0_), channel_id=1, source_target_pairs={{0,192},{1,193},{2,194},{3,195},{4,196},{5,197},{6,198},{7,199},{8... | collective-permute-start | bytes 393224 | tf_op jit(solution)/shard_map/ppermute | solution.py:21
  16.8 6.5 %collective-permute-start.2 = (bf16[1024,128]{1,0:T(8,128)(2,1)S(1)}, bf16[1024,128]{1,0:T(8,128)(2,1)S(1)}, u32[]{:S(2)}, u32[]{:S(2)}) collective-permute-start(bf16[1024,128]{1,0:T(8,128)(2,1)S(1)} %shard_map.185.refs_0_), channel_id=1, source_target_pairs={{0,16},{1,17},{2,18},{3,19},{4,20},{5,21},{6,22},{7,23},{8,56},{9,... | collective-permute-start | bytes 786440 | tf_op jit(solution)/shard_map/ppermute | solution.py:21
  23.3 8.4 %collective-permute-start.3 = (bf16[2048,128]{1,0:T(8,128)(2,1)S(1)}, bf16[2048,128]{1,0:T(8,128)(2,1)S(1)}, u32[]{:S(2)}, u32[]{:S(2)}) collective-permute-start(bf16[2048,128]{1,0:T(8,128)(2,1)S(1)} %shard_map.186.refs_0_), channel_id=1, source_target_pairs={{0,48},{1,49},{2,50},{3,51},{4,52},{5,53},{6,54},{7,55},{8,24},{9,... | collective-permute-start | bytes 1572872 | tf_op jit(solution)/shard_map/ppermute | solution.py:21
  23.4 45.4 %collective-permute-start.10 = (bf16[256,1024]{1,0:T(8,128)(2,1)}, bf16[256,1024]{1,0:T(8,128)(2,1)}, u32[]{:S(2)}, u32[]{:S(2)}) collective-permute-start(bf16[256,1024]{1,0:T(8,128)(2,1)} %param.19), channel_id=1, source_target_pairs={{0,8},{1,9},{2,10},{3,11},{4,12},{5,13},{6,14},{7,15},{8,0},{9,1},... | collective-permute-start | bytes 1572872 | tf_op jit(solution)/shard_map/ppermute | solution.py:21
  28.8 7.8 %copy-start.20 = (s32[16]{0:T(128)S(1)}, s32[16]{0:T(128)}, u32[]{:S(2)}) copy-start(s32[16]{0:T(128)} %constant.43.clone) | copy-start | bytes 196
  28.8 7.8 %copy-start.21 = (s32[16]{0:T(128)S(1)}, s32[16]{0:T(128)}, u32[]{:S(2)}) copy-start(s32[16]{0:T(128)} %constant.44.clone) | copy-start | bytes 196
  30.2 30.6 %collective-permute-start.9 = (bf16[256,1792]{1,0:T(8,128)(2,1)}, bf16[256,1792]{1,0:T(8,128)(2,1)}, u32[]{:S(2)}, u32[]{:S(2)}) collective-permute-start(bf16[256,1792]{1,0:T(8,128)(2,1)} %get-tuple-element.56), channel_id=1, source_target_pairs={{0,8},{1,9},{2,10},{3,11},{4,12},{5,13},{6,14},{7,15},{8,0},{9,1},... | collective-permute-start | bytes 2752520 | tf_op jit(solution)/shard_map/ppermute | solution.py:21
  31.8 8.4 %collective-permute-start.4 = (bf16[4096,128]{1,0:T(8,128)(2,1)S(1)}, bf16[4096,128]{1,0:T(8,128)(2,1)}, u32[]{:S(2)}, u32[]{:S(2)}) collective-permute-start(bf16[4096,128]{1,0:T(8,128)(2,1)S(1)} %shard_map.187), channel_id=1, source_target_pairs={{0,8},{1,9},{2,10},{3,11},{4,12},{5,13},{6,14},{7,15},{8,0},{9,1},... | collective-permute-start | bytes 3145736 | tf_op jit(solution)/shard_map/ppermute | solution.py:21
  36.7 2.2 %copy-start.2 = (bf16[256,8192]{1,0:T(8,128)(2,1)S(1)}, bf16[256,8192]{1,0:T(8,128)(2,1)}, u32[]{:S(2)}) copy-start(bf16[256,8192]{1,0:T(8,128)(2,1)} %refs_1_.1) | copy-start | bytes 12582916
  38.9 1.2 copy-start.19
  38.9 1.2 copy-start.16
  38.9 1.2 copy-start.17
  38.9 1.2 copy-start.13
  42.3 10.3 %copy-start.12 = (bf16[256,1024]{1,0:T(8,128)(2,1)S(1)}, bf16[256,1024]{1,0:T(8,128)(2,1)}, u32[]{:S(2)}) copy-start(bf16[256,1024]{1,0:T(8,128)(2,1)} %param.19) | copy-start | bytes 1572868
  43.1 17.7 %copy-start.8 = (bf16[256,1792]{1,0:T(8,128)(2,1)S(1)}, bf16[256,1792]{1,0:T(8,128)(2,1)}, u32[]{:S(2)}) copy-start(bf16[256,1792]{1,0:T(8,128)(2,1)} %get-tuple-element.55) | copy-start | bytes 2752516
  43.2 3.8 %collective-permute-start.5 = (bf16[128,256]{1,0:T(8,128)(2,1)S(1)}, bf16[128,256]{1,0:T(8,128)(2,1)S(1)}, u32[]{:S(2)}, u32[]{:S(2)}) collective-permute-start(bf16[128,256]{1,0:T(8,128)(2,1)S(1)} %fusion.13.refs_0_), channel_id=1, source_target_pairs={{0,1},{1,0},{2,3},{3,2},{4,5},{5,4},{6,7},{7,6},{8,9},{9,8},{10,11... | collective-permute-start | bytes 196616 | tf_op jit(solution)/shard_map/ppermute | solution.py:21
  46.9 5.2 %collective-permute-start.6 = (bf16[256,256]{1,0:T(8,128)(2,1)S(1)}, bf16[256,256]{1,0:T(8,128)(2,1)S(1)}, u32[]{:S(2)}, u32[]{:S(2)}) collective-permute-start(bf16[256,256]{1,0:T(8,128)(2,1)S(1)} %shard_map.189.refs_0_), channel_id=1, source_target_pairs={{0,2},{1,3},{2,0},{3,1},{4,6},{5,7},{6,4},{7,5},{8,14},{9,15},{10,... | collective-permute-start | bytes 393224 | tf_op jit(solution)/shard_map/ppermute | solution.py:21
  52.1 5.6 %collective-permute-start.7 = (bf16[512,256]{1,0:T(8,128)(2,1)S(1)}, bf16[512,256]{1,0:T(8,128)(2,1)S(1)}, u32[]{:S(2)}, u32[]{:S(2)}) collective-permute-start(bf16[512,256]{1,0:T(8,128)(2,1)S(1)} %shard_map.190.refs_0_), channel_id=1, source_target_pairs={{0,6},{1,7},{2,4},{3,5},{4,2},{5,3},{6,0},{7,1},{8,10},{9,11},{10,... | collective-permute-start | bytes 786440 | tf_op jit(solution)/shard_map/ppermute | solution.py:21
  57.8 4.4 %collective-permute-start.8 = (bf16[1024,256]{1,0:T(8,128)(2,1)S(1)}, bf16[1024,256]{1,0:T(8,128)(2,1)S(1)}, u32[]{:S(2)}, u32[]{:S(2)}) collective-permute-start(bf16[1024,256]{1,0:T(8,128)(2,1)S(1)} %shard_map.191.refs_1_), channel_id=1, source_target_pairs={{0,8},{1,9},{2,10},{3,11},{4,12},{5,13},{6,14},{7,15},{8,0},{9,1},... | collective-permute-start | bytes 1572872 | tf_op jit(solution)/shard_map/ppermute | solution.py:21
  62.1 6.7 %copy-start.14 = (f32[32,3584]{1,0:T(8,128)S(1)}, f32[32,3584]{1,0:T(8,128)}, u32[]{:S(2)}) copy-start(f32[32,3584]{1,0:T(8,128)} %param.21) | copy-start | bytes 1376260
  64.8 1.2 copy-start
  66.1 20.6 %collective-permute-start.11 = (bf16[512,1280]{1,0:T(8,128)(2,1)}, bf16[512,1280]{1,0:T(8,128)(2,1)}, u32[]{:S(2)}, u32[]{:S(2)}) collective-permute-start(bf16[512,1280]{1,0:T(8,128)(2,1)} %get-tuple-element.31), channel_id=1, source_target_pairs={{0,16},{1,17},{2,18},{3,19},{4,20},{5,21},{6,22},{7,23},{8,56},{9,... | collective-permute-start | bytes 3932168 | tf_op jit(solution)/shard_map/ppermute | solution.py:21
  68.9 2.2 %copy-start.9 = (f32[64,3584]{1,0:T(8,128)}, f32[64,3584]{1,0:T(8,128)S(1)}, u32[]{:S(2)}) copy-start(f32[64,3584]{1,0:T(8,128)S(1)} %constant_dynamic-update-slice_fusion.2) | copy-start | bytes 2752516
  71.1 7.6 %copy-start.15 = (bf16[512,1024]{1,0:T(8,128)(2,1)S(1)}, bf16[512,1024]{1,0:T(8,128)(2,1)}, u32[]{:S(2)}) copy-start(bf16[512,1024]{1,0:T(8,128)(2,1)} %constant_dynamic-update-slice_fusion) | copy-start | bytes 3145732
  71.1 15.6 %collective-permute-start.12 = (bf16[512,512]{1,0:T(8,128)(2,1)}, bf16[512,512]{1,0:T(8,128)(2,1)S(1)}, u32[]{:S(2)}, u32[]{:S(2)}) collective-permute-start(bf16[512,512]{1,0:T(8,128)(2,1)} %get-tuple-element.32), channel_id=1, source_target_pairs={{0,64},{1,65},{2,66},{3,67},{4,68},{5,69},{6,70},{7,71},{8,200},{9... | collective-permute-start | bytes 1572872 | tf_op jit(solution)/shard_map/ppermute | solution.py:21
  78.7 1.5 copy-start.1
  86.7 3.4 %copy-start.10 = (f32[64,3584]{1,0:T(8,128)S(1)}, f32[64,3584]{1,0:T(8,128)}, u32[]{:S(2)}) copy-start(f32[64,3584]{1,0:T(8,128)} %copy-done.9) | copy-start | bytes 2752516
  90.1 11.6 %collective-permute-start.13 = (bf16[256,1280]{1,0:T(8,128)(2,1)}, bf16[256,1280]{1,0:T(8,128)(2,1)}, u32[]{:S(2)}, u32[]{:S(2)}) collective-permute-start(bf16[256,1280]{1,0:T(8,128)(2,1)} %get-tuple-element.35), channel_id=1, source_target_pairs={{0,48},{1,49},{2,50},{3,51},{4,52},{5,53},{6,54},{7,55},{8,24},{9,... | collective-permute-start | bytes 1966088 | tf_op jit(solution)/shard_map/ppermute | solution.py:21
  90.9 17.3 %collective-permute-start.19 = (f32[64,1792]{1,0:T(8,128)}, f32[64,1792]{1,0:T(8,128)}, u32[]{:S(2)}, u32[]{:S(2)}) collective-permute-start(f32[64,1792]{1,0:T(8,128)} %constant_dynamic-slice_fusion.5), channel_id=1, source_target_pairs={{0,8},{1,9},{2,10},{3,11},{4,12},{5,13},{6,14},{7,15},{8,0},{9,1},... | collective-permute-start | bytes 1376264 | tf_op jit(solution)/shard_map/ppermute | solution.py:21
  92.0 9.8 %collective-permute-start.14 = (bf16[256,512]{1,0:T(8,128)(2,1)}, bf16[256,512]{1,0:T(8,128)(2,1)}, u32[]{:S(2)}, u32[]{:S(2)}) collective-permute-start(bf16[256,512]{1,0:T(8,128)(2,1)} %get-tuple-element.36), channel_id=1, source_target_pairs={{0,192},{1,193},{2,194},{3,195},{4,196},{5,197},{6,198},{7,199},{8... | collective-permute-start | bytes 786440 | tf_op jit(solution)/shard_map/ppermute | solution.py:21
  104.1 10.2 %collective-permute-start.15 = (bf16[128,1280]{1,0:T(8,128)(2,1)S(1)}, bf16[128,1280]{1,0:T(8,128)(2,1)S(1)}, u32[]{:S(2)}, u32[]{:S(2)}) collective-permute-start(bf16[128,1280]{1,0:T(8,128)(2,1)S(1)} %get-tuple-element.39), channel_id=1, source_target_pairs={{0,64},{1,65},{2,66},{3,67},{4,68},{5,69},{6,70},{7,71},{8,200},{9... | collective-permute-start | bytes 983048 | tf_op jit(solution)/shard_map/ppermute | solution.py:21
  107.8 5.2 %collective-permute-start.16 = (bf16[128,512]{1,0:T(8,128)(2,1)S(1)}, bf16[128,512]{1,0:T(8,128)(2,1)S(1)}, u32[]{:S(2)}, u32[]{:S(2)}) collective-permute-start(bf16[128,512]{1,0:T(8,128)(2,1)S(1)} %get-tuple-element.40), channel_id=1, source_target_pairs={{0,16},{1,17},{2,18},{3,19},{4,20},{5,21},{6,22},{7,23},{8,56},{9,... | collective-permute-start | bytes 393224 | tf_op jit(solution)/shard_map/ppermute | solution.py:21
  114.3 5.2 %collective-permute-start.17 = (bf16[64,1280]{1,0:T(8,128)(2,1)S(1)}, bf16[64,1280]{1,0:T(8,128)(2,1)S(1)}, u32[]{:S(2)}, u32[]{:S(2)}) collective-permute-start(bf16[64,1280]{1,0:T(8,128)(2,1)S(1)} %get-tuple-element.43), channel_id=1, source_target_pairs={{0,192},{1,193},{2,194},{3,195},{4,196},{5,197},{6,198},{7,199},{8... | collective-permute-start | bytes 491528 | tf_op jit(solution)/shard_map/ppermute | solution.py:21
  115.7 3.1 %collective-permute-start.18 = (bf16[64,512]{1,0:T(8,128)(2,1)S(1)}, bf16[64,512]{1,0:T(8,128)(2,1)S(1)}, u32[]{:S(2)}, u32[]{:S(2)}) collective-permute-start(bf16[64,512]{1,0:T(8,128)(2,1)S(1)} %get-tuple-element.44), channel_id=1, source_target_pairs={{0,48},{1,49},{2,50},{3,51},{4,52},{5,53},{6,54},{7,55},{8,24},{9,... | collective-permute-start | bytes 196616 | tf_op jit(solution)/shard_map/ppermute | solution.py:21
  120.7 20.8 %copy-start.5 = (f32[64,1792]{1,0:T(8,128)}, f32[64,1792]{1,0:T(8,128)S(1)}, u32[]{:S(2)}) copy-start(f32[64,1792]{1,0:T(8,128)S(1)} %get-tuple-element.46) | copy-start | bytes 1376260
  120.7 5.4 %collective-permute-start.21 = (bf16[64,1280]{1,0:T(8,128)(2,1)S(1)}, bf16[64,1280]{1,0:T(8,128)(2,1)S(1)}, u32[]{:S(2)}, u32[]{:S(2)}) collective-permute-start(bf16[64,1280]{1,0:T(8,128)(2,1)S(1)} %get-tuple-element.47.refs_0_), channel_id=1, source_target_pairs={{0,192},{1,193},{2,194},{3,195},{4,196},{5,197},{6,198},{7,199},{8... | collective-permute-start | bytes 491528 | tf_op jit(solution)/shard_map/ppermute | solution.py:21
  121.9 3.5 %collective-permute-start.22 = (bf16[64,512]{1,0:T(8,128)(2,1)S(1)}, bf16[64,512]{1,0:T(8,128)(2,1)S(1)}, u32[]{:S(2)}, u32[]{:S(2)}) collective-permute-start(bf16[64,512]{1,0:T(8,128)(2,1)S(1)} %get-tuple-element.48.refs_2_), channel_id=1, source_target_pairs={{0,48},{1,49},{2,50},{3,51},{4,52},{5,53},{6,54},{7,55},{8,24},{9,... | collective-permute-start | bytes 196616 | tf_op jit(solution)/shard_map/ppermute | solution.py:21
  126.1 14.6 %collective-permute-start.23 = (bf16[128,1280]{1,0:T(8,128)(2,1)S(1)}, bf16[128,1280]{1,0:T(8,128)(2,1)S(1)}, u32[]{:S(2)}, u32[]{:S(2)}) collective-permute-start(bf16[128,1280]{1,0:T(8,128)(2,1)S(1)} %get-tuple-element.49.refs_0_), channel_id=1, source_target_pairs={{0,64},{1,65},{2,66},{3,67},{4,68},{5,69},{6,70},{7,71},{8,200},{9... | collective-permute-start | bytes 983048 | tf_op jit(solution)/shard_map/ppermute | solution.py:21
  131.8 6.0 %collective-permute-start.24 = (bf16[128,512]{1,0:T(8,128)(2,1)S(1)}, bf16[128,512]{1,0:T(8,128)(2,1)S(1)}, u32[]{:S(2)}, u32[]{:S(2)}) collective-permute-start(bf16[128,512]{1,0:T(8,128)(2,1)S(1)} %get-tuple-element.50.refs_2_), channel_id=1, source_target_pairs={{0,16},{1,17},{2,18},{3,19},{4,20},{5,21},{6,22},{7,23},{8,56},{9,... | collective-permute-start | bytes 393224 | tf_op jit(solution)/shard_map/ppermute | solution.py:21
  141.5 13.4 %collective-permute-start.25 = (bf16[256,1280]{1,0:T(8,128)(2,1)S(1)}, bf16[256,1280]{1,0:T(8,128)(2,1)S(1)}, u32[]{:S(2)}, u32[]{:S(2)}) collective-permute-start(bf16[256,1280]{1,0:T(8,128)(2,1)S(1)} %get-tuple-element.51.refs_0_), channel_id=1, source_target_pairs={{0,48},{1,49},{2,50},{3,51},{4,52},{5,53},{6,54},{7,55},{8,24},{9,... | collective-permute-start | bytes 1966088 | tf_op jit(solution)/shard_map/ppermute | solution.py:21
  141.5 13.4 %collective-permute-start.26 = (bf16[256,512]{1,0:T(8,128)(2,1)}, bf16[256,512]{1,0:T(8,128)(2,1)}, u32[]{:S(2)}, u32[]{:S(2)}) collective-permute-start(bf16[256,512]{1,0:T(8,128)(2,1)} %get-tuple-element.52.refs_2_), channel_id=1, source_target_pairs={{0,192},{1,193},{2,194},{3,195},{4,196},{5,197},{6,198},{7,199},{8... | collective-permute-start | bytes 786440 | tf_op jit(solution)/shard_map/ppermute | solution.py:21
  144.6 14.6 %copy-start.6 = (f32[64,1792]{1,0:T(8,128)S(1)}, f32[64,1792]{1,0:T(8,128)}, u32[]{:S(2)}) copy-start(f32[64,1792]{1,0:T(8,128)} %copy-done.5) | copy-start | bytes 1376260
  156.1 36.7 %collective-permute-start.27 = (bf16[512,1280]{1,0:T(8,128)(2,1)S(1)}, bf16[512,1280]{1,0:T(8,128)(2,1)S(1)}, u32[]{:S(2)}, u32[]{:S(2)}) collective-permute-start(bf16[512,1280]{1,0:T(8,128)(2,1)S(1)} %get-tuple-element.53.refs_2_), channel_id=1, source_target_pairs={{0,16},{1,17},{2,18},{3,19},{4,20},{5,21},{6,22},{7,23},{8,56},{9,... | collective-permute-start | bytes 3932168 | tf_op jit(solution)/shard_map/ppermute | solution.py:21
  159.3 19.8 %collective-permute-start.20 = (f32[64,1792]{1,0:T(8,128)S(1)}, f32[64,1792]{1,0:T(8,128)S(1)}, u32[]{:S(2)}, u32[]{:S(2)}) collective-permute-start(f32[64,1792]{1,0:T(8,128)S(1)} %pad_maximum_fusion.1), channel_id=1, source_target_pairs={{0,8},{1,9},{2,10},{3,11},{4,12},{5,13},{6,14},{7,15},{8,0},{9,1},... | collective-permute-start | bytes 1376264 | tf_op jit(solution)/shard_map/ppermute | solution.py:21
  177.1 15.6 %collective-permute-start.28 = (bf16[512,512]{1,0:T(8,128)(2,1)S(1)}, bf16[512,512]{1,0:T(8,128)(2,1)S(1)}, u32[]{:S(2)}, u32[]{:S(2)}) collective-permute-start(bf16[512,512]{1,0:T(8,128)(2,1)S(1)} %get-tuple-element.54.refs_3_), channel_id=1, source_target_pairs={{0,64},{1,65},{2,66},{3,67},{4,68},{5,69},{6,70},{7,71},{8,200},{9... | collective-permute-start | bytes 1572872 | tf_op jit(solution)/shard_map/ppermute | solution.py:21
  193.4 4.1 %collective-permute-start.29 = (bf16[256,1792]{1,0:T(8,128)(2,1)S(1)}, bf16[256,1792]{1,0:T(8,128)(2,1)S(1)}, u32[]{:S(2)}, u32[]{:S(2)}) collective-permute-start(bf16[256,1792]{1,0:T(8,128)(2,1)S(1)} %shard_map.203), channel_id=1, source_target_pairs={{0,8},{1,9},{2,10},{3,11},{4,12},{5,13},{6,14},{7,15},{8,0},{9,1},... | collective-permute-start | bytes 2752520 | tf_op jit(solution)/shard_map/ppermute | solution.py:21
  (4 other events, 3.8 us)

commit v2 on v1

--- a/solution.py
+++ b/solution.py
@@ -47,7 +47,7 @@
     )
 
 
-def call(kernel, outs, args, flops=0, vmem=8, scratch=(), smem=0, after=()):
+def call(kernel, outs, args, flops=0, vmem=16, scratch=(), smem=0, after=()):
     moved = sum(a.size * a.dtype.itemsize for a in args)
     moved += sum(o.size * o.dtype.itemsize for o in outs)
     specs = [
@@ -104,7 +104,7 @@
 def reorder(array, index, width):
     outs = [shape(array.shape[0], array.shape[1], array.dtype)]
     return call(
-        functools.partial(reorder_kernel, width), outs, [index, array], vmem=8, smem=1
+        functools.partial(reorder_kernel, width), outs, [index, array], vmem=24, smem=1
     )[0]
 
 
@@ -116,9 +116,8 @@
         blocks = out_ref.shape[0] // block
         for k in range(blocks):
             row = slice(k * block, (k + 1) * block)
-            start = pl.multiple_of(index_ref[0, part * blocks + k] * block, block)
+            start = pl.multiple_of(index_ref[part * blocks + k] * block, block)
             chosen[row, :tokens] = own_ref[pl.ds(start, block), :]
-            start = pl.multiple_of(index_ref[1, part * blocks + k] * block, block)
             chosen[row, tokens:] = other_ref[pl.ds(start, block), :]
         width = out_ref.shape[1]
         out_ref[...] = jnp.dot(
@@ -133,7 +132,7 @@
         [shape(rows, w, kind) for w in widths],
         [index, own, other, grads],
         flops=2 * rows * grads.size,
-        vmem=12,
+        vmem=24,
         scratch=[pltpu.VMEM((rows, 2 * own.shape[1]), BF)],
         smem=1,
         after=after,
@@ -174,12 +173,22 @@
         )
 
 
-def adam(kept, got, first, second):
+def adam(kept, got, first, second, after):
     outs = [shape(*first.shape, F32)] * 2 + [shape(*k.shape, BF) for k in kept]
     result = call(
-        functools.partial(adam_kernel, len(kept)), outs, [*kept, *got, first, second]
+        functools.partial(adam_kernel, len(kept)),
+        outs,
+        [*kept, *got, first, second],
+        after=after,
     )
     return result[0], result[1], result[2:]
+
+
+def pick_kernel(which_ref, first_ref, second_ref, out_ref):
+    rows = out_ref.shape[0] // 2
+    start = pl.multiple_of(which_ref[0] * rows, rows)
+    out_ref[:rows, :] = first_ref[pl.ds(start, rows), :]
+    out_ref[rows:, :] = second_ref[pl.ds(start, rows), :]
 
 
 def early_kernel(count, *refs):
@@ -221,8 +230,8 @@
     rank = projector.shape[1]
     block = rank // 16
     column_count = rank // 8
-    wide = half * 5 // 7
-    widths = (wide, half - wide)
+    wide = half * 5 // 14
+    widths = (wide, wide, half - 2 * wide)
     rows = first_moment.shape[0]
 
     def my_half(array):
@@ -232,14 +241,11 @@
         return lax.dynamic_slice_in_dim(array, (1 - core) * half, half, 1)
 
     columns = lax.dynamic_slice_in_dim(projector, tp_place * column_count, column_count, 1)
-    column_orders = ([8, 24, 2, 6], [24, 8, 6, 2])
-    for masks in zip(*column_orders):
-        columns = stack([[columns, swap(columns, "fsdp", masks)]])[0]
+    for masks in ((8, 16, 24), (2, 4, 6)):
+        columns = stack([[columns] + [swap(columns, "fsdp", (m, m)) for m in masks]])[0]
     columns_other = swap_core(columns)
-    order = [doubled(o) for o in column_orders]
-    index = jnp.concatenate(
-        [place ^ table(core, order), place ^ 1 ^ table(1 - core, order)]
-    )
+    order = jnp.array([x + z for x in (0, 2, 4, 6) for z in (0, 8, 16, 24)], jnp.int32)
+    index = jnp.concatenate([place ^ order, place ^ 1 ^ order])
     act = reorder(activations, index, projector.shape[0])
     depth = columns.shape[0]
     dims = (((0,), (1,)), ((), ()))
@@ -247,17 +253,9 @@
     own = own + lax.dot_general(columns_other, act[:, depth:], dims, preferred_element_type=F32)
     own = own.astype(BF)
 
-    coords = own
-    for masks in ((1, 1), (2, 6), (6, 2)):
-        coords = stack([[coords, swap(coords, "tp", masks)]])[0]
+    coords = stack([[own, swap(own, "tp", (1, 1))]])[0]
+    coords = stack([[coords] + [swap(coords, "tp", (m, m)) for m in (2, 4, 6)]])[0]
     coords_other = swap_core(coords)
-
-    def position(wanted, which):
-        part = tp_place ^ (wanted >> 1)
-        high = part >> 2
-        mixed = ((part >> 1) ^ high) & 1
-        upper = jnp.where(which == 0, 2 * mixed + 4 * high, 2 * high + 4 * mixed)
-        return 2 * ((part & 1) + upper) + (wanted & 1)
 
     grads = jnp.concatenate(
         [my_half(grad_output), swap_core(other_half(grad_output))], axis=0
@@ -269,14 +267,18 @@
     second = by_core(core, moments_own[rows:], moments_other[rows:], 0)
     both = jnp.concatenate([projector, swap_core(projector)], axis=0)
 
-    sum_orders = (([1, 3, 4, 12], [3, 1, 12, 4]), ([4, 12, 1, 3], [12, 4, 3, 1]))
+    sum_orders = (
+        ([1, 3, 4, 12], [1, 3, 4, 12]),
+        ([3, 1, 12, 4], [3, 1, 12, 4]),
+        ([4, 12, 1, 3], [12, 4, 3, 1]),
+    )
     back_orders = [[o[::-1] for o in orders] for orders in sum_orders]
     keep_index, send_index = [], []
     for orders in sum_orders:
         wanted = chip ^ table(core, [doubled(o[::-1]) for o in orders])
-        places = jnp.stack([position(wanted, core), position(wanted, 1 - core)])
-        keep_index.append(places[:, :8])
-        send_index.append(places[:, 8:])
+        position = 2 * (tp_place ^ (wanted >> 1)) + (wanted & 1)
+        keep_index.append(position[:8])
+        send_index.append(position[8:])
     ranks = jnp.arange(rank, dtype=jnp.int32)
     factors = []
     for orders in back_orders:
@@ -291,21 +293,15 @@
         ]
 
     arrays = (coords, coords_other, grads, rank // 2, widths, block)
-    sent = partial_sums(jnp.concatenate(send_index, axis=1), *arrays, BF)
-    kept = partial_sums(jnp.concatenate(keep_index, axis=1), *arrays, F32, after=factors)
+    sent = partial_sums(jnp.concatenate(send_index), *arrays, BF)
+    kept = partial_sums(jnp.concatenate(keep_index), *arrays, F32)
     for stage in range(3):
         kept, sent = halve(kept, exchange(sent, sum_orders, stage))
     got = exchange(sent, sum_orders, 3)
-    new_first, new_second, parts = adam(kept, got, first, second)
+    new_first, new_second, parts = adam(kept, got, first, second, factors)
 
     def rows_of(array, which):
         return lax.dynamic_slice_in_dim(array, which * rows, rows, 0)
-
-    states_other = swap_core(
-        jnp.concatenate([rows_of(new_first, 1 - core), rows_of(new_second, 1 - core)], axis=0)
-    )
-    out_first = by_core(core, rows_of(new_first, core), states_other[:rows], 1)
-    out_second = by_core(core, rows_of(new_second, core), states_other[rows:], 1)
 
     for stage in range(4):
         got = exchange(parts, back_orders, stage)
@@ -318,7 +314,7 @@
         [shape(both.shape[0], half, F32)],
         [*factors, *parts],
         flops=flops,
-        vmem=12,
+        vmem=32,
     )[0]
     late = [
         call(
@@ -326,11 +322,23 @@
             [shape(tokens, half, BF)],
             [*factors, *got, early],
             flops=flops // 2,
-            vmem=12,
+            vmem=32,
         )[0]
         for row in (tokens, 0)
     ]
-    update = by_core(core, late[1], swap_core(late[0]), 1)
+    late_other = swap_core(late[0])
+    states_other = swap_core(
+        call(
+            pick_kernel,
+            [shape(2 * rows, half, F32)],
+            [(1 - core)[None], new_first, new_second],
+            smem=1,
+            after=[late[0]],
+        )[0]
+    )
+    out_first = by_core(core, rows_of(new_first, core), states_other[:rows], 1)
+    out_second = by_core(core, rows_of(new_second, core), states_other[rows:], 1)
+    update = by_core(core, late[1], late_other, 1)
     return (out_first, out_second, update)
 
 

time: 201 us -> 184 us (0.915)
  local copies, waits for them, and re-layouts: 16.2 us -> 10 us
  waiting for transfers between devices: 73.8 us -> 69.2 us
  starting transfers between devices: 82 us -> 78.4 us
    ppermute x30 -> x41, waiting for transfers between devices: 73.8 us -> 69.2 us  [swap(): lax.ppermute(array, ('fsdp', 'tp'), [(i, i ^ scale * masks[i // inner % 2...]
    ppermute x30 -> x41, starting transfers between devices: 82 us -> 78.4 us  [swap(): lax.ppermute(array, ('fsdp', 'tp'), [(i, i ^ scale * masks[i // inner % 2...]
    unnamed x46 -> x30, local copies, waits for them, and re-layouts: 7.13 us -> 3.84 us
    pallas_call x20 -> x18, Pallas kernels: 14.4 us -> 14.3 us  [call(): pl.pallas_call(body, out_shape=list(outs), in_specs=specs, out_specs=[pl....]
  transfers between devices with their start and end apart: 30 -> 41, of which waited for: 20 -> 19; matrix products, arithmetic and copies ran while one was open for 10% -> 8% of each run, Pallas kernels for 4% -> 5%
where the time goes in v2:
time: 184 us
  starting transfers between devices  78.4 us (43%)
  waiting for transfers between devices  69.2 us (38%)
  Pallas kernels  14.3 us (8%)
  local copies, waits for them, and re-layouts  10 us (5%)
  matrix products  5.63 us (3%)
  other arithmetic  4.88 us (3%)
    ppermute x41, starting transfers between devices, swap(): lax.ppermute(array, ('fsdp', 'tp'), [(i, i ^ scale * masks[i // inner % 2...  78.4 us
    ppermute x41, waiting for transfers between devices, swap(): lax.ppermute(array, ('fsdp', 'tp'), [(i, i ^ scale * masks[i // inner % 2...  69.2 us
    pallas_call x18, Pallas kernels, call(): pl.pallas_call(body, out_shape=list(outs), in_specs=specs, out_specs=[pl....  14.3 us
    dot_general x3, matrix products, body(): factors.append(jnp.dot(both, choose, preferred_element_type=F32).astype(BF))  3.94 us
    unnamed x30, local copies, waits for them, and re-layouts  3.84 us
  transfers between devices with their start and end apart: 41, of which 19 were waited for; matrix products, arithmetic and copies ran while one was open for 8% of the time, Pallas kernels for 5%

profile of v2, /device:TPU:1, one launch (start us, length us, event | category | flops | bytes accessed | tf_op | source)
XLA Modules:
  0.0 183.6 jit_solution(18108541734459563857)
XLA Ops:
  1.6 3.8 %collective-permute-start = (bf16[256,128]{1,0:T(8,128)(2,1)S(1)}, bf16[256,128]{1,0:T(8,128)(2,1)S(1)}, u32[]{:S(2)}, u32[]{:S(2)}) collective-permute-start(bf16[256,128]{1,0:T(8,128)(2,1)S(1)} %constant_dynamic-slice_fusion.6.refs_0_), channel_id=1, source_target_pairs={{0,64},{1,65},{2,66},{3,67},{4,68},{5,69},{6,70},{7,71},{8,72},{9,... | collective-permute-start | bytes 196616 | tf_op jit(solution)/shard_map/ppermute | solution.py:21
  5.4 5.1 %collective-permute-start.1 = (bf16[256,128]{1,0:T(8,128)(2,1)S(1)}, bf16[256,128]{1,0:T(8,128)(2,1)S(1)}, u32[]{:S(2)}, u32[]{:S(2)}) collective-permute-start(bf16[256,128]{1,0:T(8,128)(2,1)S(1)} %constant_dynamic-slice_fusion.6.refs_0_), channel_id=1, source_target_pairs={{0,128},{1,129},{2,130},{3,131},{4,132},{5,133},{6,134},{7,135},{8... | collective-permute-start | bytes 196616 | tf_op jit(solution)/shard_map/ppermute | solution.py:21
  10.5 1.2 collective-permute-start.26
  11.7 2.5 %constant_dynamic-slice_fusion.5 = (bf16[256,1792]{1,0:T(8,128)(2,1)S(1)}, bf16[256,1792]{1,0:T(8,128)(2,1)}) fusion(bf16[256,3584]{1,0:T(8,128)(2,1)} %param.19, s32[]{:T(128)S(6)} %select_n.81, s32[]{:T(128)S(6)} %select_n.82), kind=kLoop, calls=%fused_computation.36 | loop fusion | bytes 3670024 | tf_op jit(solution)/shard_map/dynamic_slice | solution.py:238
  14.4 1.6 collective-permute-done.2.refs_3_
  16.0 1.3 collective-permute-start.3
  17.3 2.5 %collective-permute-start.4 = (bf16[1024,128]{1,0:T(8,128)(2,1)S(1)}, bf16[1024,128]{1,0:T(8,128)(2,1)S(1)}, u32[]{:S(2)}, u32[]{:S(2)}) collective-permute-start(bf16[1024,128]{1,0:T(8,128)(2,1)S(1)} %shard_map.193.refs_0_), channel_id=1, source_target_pairs={{0,32},{1,33},{2,34},{3,35},{4,36},{5,37},{6,38},{7,39},{8,40},{9,... | collective-permute-start | bytes 786440 | tf_op jit(solution)/shard_map/ppermute | solution.py:21
  20.0 2.2 %copy-done = bf16[256,8192]{1,0:T(8,128)(2,1)S(1)} copy-done((bf16[256,8192]{1,0:T(8,128)(2,1)S(1)}, bf16[256,8192]{1,0:T(8,128)(2,1)}, u32[]{:S(2)}) %copy-start) | copy-done | bytes 4194328
  23.5 6.1 %collective-permute-done.4.refs_2_ = bf16[1024,128]{1,0:T(8,128)(2,1)S(1)} collective-permute-done((bf16[1024,128]{1,0:T(8,128)(2,1)S(1)}, bf16[1024,128]{1,0:T(8,128)(2,1)S(1)}, u32[]{:S(2)}, u32[]{:S(2)}) %collective-permute-start.4) | collective-permute-done | bytes 262176 | tf_op jit(solution)/shard_map/ppermute | solution.py:21
  29.6 3.5 %collective-permute-done.5.refs_3_ = bf16[1024,128]{1,0:T(8,128)(2,1)S(1)} collective-permute-done((bf16[1024,128]{1,0:T(8,128)(2,1)S(1)}, bf16[1024,128]{1,0:T(8,128)(2,1)S(1)}, u32[]{:S(2)}, u32[]{:S(2)}) %collective-permute-start.5) | collective-permute-done | bytes 262176 | tf_op jit(solution)/shard_map/ppermute | solution.py:21
  33.2 2.3 %collective-permute-start.6 = (bf16[4096,128]{1,0:T(8,128)(2,1)S(1)}, bf16[4096,128]{1,0:T(8,128)(2,1)S(1)}, u32[]{:S(2)}, u32[]{:S(2)}) collective-permute-start(bf16[4096,128]{1,0:T(8,128)(2,1)S(1)} %shard_map.194), channel_id=1, source_target_pairs={{0,8},{1,9},{2,10},{3,11},{4,12},{5,13},{6,14},{7,15},{8,0},{9,1},... | collective-permute-start | bytes 3145736 | tf_op jit(solution)/shard_map/ppermute | solution.py:21
  35.7 2.1 %collective-permute-done.6 = bf16[4096,128]{1,0:T(8,128)(2,1)S(1)} collective-permute-done((bf16[4096,128]{1,0:T(8,128)(2,1)S(1)}, bf16[4096,128]{1,0:T(8,128)(2,1)S(1)}, u32[]{:S(2)}, u32[]{:S(2)}) %collective-permute-start.6) | collective-permute-done | bytes 1048608 | tf_op jit(solution)/shard_map/ppermute | solution.py:21
  40.4 2.3 %collective-permute-done.7.refs_1_ = bf16[128,256]{1,0:T(8,128)(2,1)S(1)} collective-permute-done((bf16[128,256]{1,0:T(8,128)(2,1)S(1)}, bf16[128,256]{1,0:T(8,128)(2,1)S(1)}, u32[]{:S(2)}, u32[]{:S(2)}) %collective-permute-start.7) | collective-permute-done | bytes 65568 | tf_op jit(solution)/shard_map/ppermute | solution.py:21
  42.7 2.8 %collective-permute-start.10 = (bf16[256,256]{1,0:T(8,128)(2,1)S(1)}, bf16[256,256]{1,0:T(8,128)(2,1)S(1)}, u32[]{:S(2)}, u32[]{:S(2)}) collective-permute-start(bf16[256,256]{1,0:T(8,128)(2,1)S(1)} %shard_map.196.refs_0_), channel_id=1, source_target_pairs={{0,6},{1,7},{2,4},{3,5},{4,2},{5,3},{6,0},{7,1},{8,14},{9,15},{10,... | collective-permute-start | bytes 393224 | tf_op jit(solution)/shard_map/ppermute | solution.py:21
  45.5 1.3 collective-permute-start.9
  47.9 3.4 %collective-permute-start.25 = (f32[64,1792]{1,0:T(8,128)S(1)}, f32[64,1792]{1,0:T(8,128)}, u32[]{:S(2)}, u32[]{:S(2)}) collective-permute-start(f32[64,1792]{1,0:T(8,128)S(1)} %constant_dynamic-slice_fusion.3), channel_id=1, source_target_pairs={{0,8},{1,9},{2,10},{3,11},{4,12},{5,13},{6,14},{7,15},{8,0},{9,1},... | collective-permute-start | bytes 1376264 | tf_op jit(solution)/shard_map/ppermute | solution.py:21
  51.9 2.5 %collective-permute-start.11 = (bf16[1024,256]{1,0:T(8,128)(2,1)S(1)}, bf16[1024,256]{1,0:T(8,128)(2,1)S(1)}, u32[]{:S(2)}, u32[]{:S(2)}) collective-permute-start(bf16[1024,256]{1,0:T(8,128)(2,1)S(1)} %shard_map.197.refs_1_), channel_id=1, source_target_pairs={{0,8},{1,9},{2,10},{3,11},{4,12},{5,13},{6,14},{7,15},{8,0},{9,1},... | collective-permute-start | bytes 1572872 | tf_op jit(solution)/shard_map/ppermute | solution.py:21
  54.9 1.3 pad_maximum_fusion.refs_3_
  56.2 1.8 shard_map.199
  58.6 4.3 %collective-permute-start.15 = (bf16[512,512]{1,0:T(8,128)(2,1)S(1)}, bf16[512,512]{1,0:T(8,128)(2,1)S(1)}, u32[]{:S(2)}, u32[]{:S(2)}) collective-permute-start(bf16[512,512]{1,0:T(8,128)(2,1)S(1)} %get-tuple-element.46), channel_id=1, source_target_pairs={{0,64},{1,65},{2,66},{3,67},{4,68},{5,69},{6,70},{7,71},{8,200},{9... | collective-permute-start | bytes 1572872 | tf_op jit(solution)/shard_map/ppermute | solution.py:21
  64.1 1.8 shard_map.198
  65.9 8.8 %collective-permute-done.15.refs_5_ = bf16[512,512]{1,0:T(8,128)(2,1)S(1)} collective-permute-done((bf16[512,512]{1,0:T(8,128)(2,1)S(1)}, bf16[512,512]{1,0:T(8,128)(2,1)S(1)}, u32[]{:S(2)}, u32[]{:S(2)}) %collective-permute-start.15) | collective-permute-done | bytes 524320 | tf_op jit(solution)/shard_map/ppermute | solution.py:21
  76.0 1.5 collective-permute-start.16
  78.8 1.9 %collective-permute-start.18 = (bf16[256,512]{1,0:T(8,128)(2,1)S(1)}, bf16[256,512]{1,0:T(8,128)(2,1)S(1)}, u32[]{:S(2)}, u32[]{:S(2)}) collective-permute-start(bf16[256,512]{1,0:T(8,128)(2,1)S(1)} %get-tuple-element.52), channel_id=1, source_target_pairs={{0,192},{1,193},{2,194},{3,195},{4,196},{5,197},{6,198},{7,199},{8... | collective-permute-start | bytes 786440 | tf_op jit(solution)/shard_map/ppermute | solution.py:21
  80.6 1.3 fusion.10.refs_10_.refs_2_
  81.9 6.2 %collective-permute-done.18.refs_5_ = bf16[256,512]{1,0:T(8,128)(2,1)S(1)} collective-permute-done((bf16[256,512]{1,0:T(8,128)(2,1)S(1)}, bf16[256,512]{1,0:T(8,128)(2,1)S(1)}, u32[]{:S(2)}, u32[]{:S(2)}) %collective-permute-start.18) | collective-permute-done | bytes 262176 | tf_op jit(solution)/shard_map/ppermute | solution.py:21
  89.2 4.3 %collective-permute-start.20 = (bf16[128,640]{1,0:T(8,128)(2,1)S(1)}, bf16[128,640]{1,0:T(8,128)(2,1)S(1)}, u32[]{:S(2)}, u32[]{:S(2)}) collective-permute-start(bf16[128,640]{1,0:T(8,128)(2,1)S(1)} %get-tuple-element.57), channel_id=1, source_target_pairs={{0,192},{1,193},{2,194},{3,195},{4,196},{5,197},{6,198},{7,199},{8... | collective-permute-start | bytes 491528 | tf_op jit(solution)/shard_map/ppermute | solution.py:21
  93.5 1.6 collective-permute-start.21
  95.2 1.3 fusion.11.refs_9_.refs_1_
  96.5 2.4 %collective-permute-done.21.refs_5_ = bf16[128,512]{1,0:T(8,128)(2,1)S(1)} collective-permute-done((bf16[128,512]{1,0:T(8,128)(2,1)S(1)}, bf16[128,512]{1,0:T(8,128)(2,1)S(1)}, u32[]{:S(2)}, u32[]{:S(2)}) %collective-permute-start.21) | collective-permute-done | bytes 131104 | tf_op jit(solution)/shard_map/ppermute | solution.py:21
  98.9 3.5 %collective-permute-start.22 = (bf16[64,640]{1,0:T(8,128)(2,1)S(1)}, bf16[64,640]{1,0:T(8,128)(2,1)S(1)}, u32[]{:S(2)}, u32[]{:S(2)}) collective-permute-start(bf16[64,640]{1,0:T(8,128)(2,1)S(1)} %get-tuple-element.62), channel_id=1, source_target_pairs={{0,192},{1,193},{2,194},{3,195},{4,196},{5,197},{6,198},{7,199},{8... | collective-permute-start | bytes 245768 | tf_op jit(solution)/shard_map/ppermute | solution.py:21
  103.6 1.3 fusion.12.refs_8_.refs_0_
  105.6 1.6 collective-permute-done.23.refs_4_
  111.2 2.4 %collective-permute-done.29.refs_5_ = bf16[64,512]{1,0:T(8,128)(2,1)S(1)} collective-permute-done((bf16[64,512]{1,0:T(8,128)(2,1)S(1)}, bf16[64,512]{1,0:T(8,128)(2,1)S(1)}, u32[]{:S(2)}, u32[]{:S(2)}) %collective-permute-start.29) | collective-permute-done | bytes 65568 | tf_op jit(solution)/shard_map/ppermute | solution.py:21
  113.5 1.9 %collective-permute-done.27.refs_1_ = bf16[64,640]{1,0:T(8,128)(2,1)S(1)} collective-permute-done((bf16[64,640]{1,0:T(8,128)(2,1)S(1)}, bf16[64,640]{1,0:T(8,128)(2,1)S(1)}, u32[]{:S(2)}, u32[]{:S(2)}) %collective-permute-start.27) | collective-permute-done | bytes 81952 | tf_op jit(solution)/shard_map/ppermute | solution.py:21
  116.3 2.4 %collective-permute-start.31 = (bf16[128,640]{1,0:T(8,128)(2,1)S(1)}, bf16[128,640]{1,0:T(8,128)(2,1)S(1)}, u32[]{:S(2)}, u32[]{:S(2)}) collective-permute-start(bf16[128,640]{1,0:T(8,128)(2,1)S(1)} %get-tuple-element.71.refs_2_), channel_id=1, source_target_pairs={{0,192},{1,193},{2,194},{3,195},{4,196},{5,197},{6,198},{7,199},{8... | collective-permute-start | bytes 491528 | tf_op jit(solution)/shard_map/ppermute | solution.py:21
  119.4 4.3 %collective-permute-done.32.refs_5_ = bf16[128,512]{1,0:T(8,128)(2,1)S(1)} collective-permute-done((bf16[128,512]{1,0:T(8,128)(2,1)S(1)}, bf16[128,512]{1,0:T(8,128)(2,1)S(1)}, u32[]{:S(2)}, u32[]{:S(2)}) %collective-permute-start.32) | collective-permute-done | bytes 131104 | tf_op jit(solution)/shard_map/ppermute | solution.py:21
  124.2 1.4 collective-permute-start.33
  125.7 2.4 %collective-permute-start.35 = (bf16[256,512]{1,0:T(8,128)(2,1)S(1)}, bf16[256,512]{1,0:T(8,128)(2,1)S(1)}, u32[]{:S(2)}, u32[]{:S(2)}) collective-permute-start(bf16[256,512]{1,0:T(8,128)(2,1)S(1)} %get-tuple-element.75.refs_4_), channel_id=1, source_target_pairs={{0,192},{1,193},{2,194},{3,195},{4,196},{5,197},{6,198},{7,199},{8... | collective-permute-start | bytes 786440 | tf_op jit(solution)/shard_map/ppermute | solution.py:21
  128.0 8.5 %collective-permute-done.35.refs_5_ = bf16[256,512]{1,0:T(8,128)(2,1)S(1)} collective-permute-done((bf16[256,512]{1,0:T(8,128)(2,1)S(1)}, bf16[256,512]{1,0:T(8,128)(2,1)S(1)}, u32[]{:S(2)}, u32[]{:S(2)}) %collective-permute-start.35) | collective-permute-done | bytes 262176 | tf_op jit(solution)/shard_map/ppermute | solution.py:21
  136.5 1.4 shard_map.206
  138.2 1.6 collective-permute-start.37
  140.4 2.7 %shard_map.207.refs_6_ = f32[512,1792]{1,0:T(8,128)S(1)} custom-call(bf16[512,1024]{1,0:T(8,128)(2,1)S(1)} %fusion.12.refs_8_.refs_0_, bf16[512,1024]{1,0:T(8,128)(2,1)S(1)} %fusion.11.refs_9_.refs_1_, bf16[512,1024]{1,0:T(8,128)(2,1)S(1)} %fusion.10.refs_10_.refs_2_, bf16[512,640]{1,0:T(8,128)(2,1)} %get-tuple-element.76.refs_3_, ...), custom_call_target="tpu_custom_call" | custom-call | flops 939524096 | bytes 8650752 | tf_op jit(solution)/shard_map/pallas_call | solution.py:63
  143.1 13.7 %collective-permute-done.38.refs_5_ = bf16[512,512]{1,0:T(8,128)(2,1)} collective-permute-done((bf16[512,512]{1,0:T(8,128)(2,1)}, bf16[512,512]{1,0:T(8,128)(2,1)}, u32[]{:S(2)}, u32[]{:S(2)}) %collective-permute-start.38) | collective-permute-done | bytes 524320 | tf_op jit(solution)/shard_map/ppermute | solution.py:21
  156.8 2.1 %shard_map.208.refs_3_ = bf16[256,1792]{1,0:T(8,128)(2,1)S(1)} custom-call(bf16[512,1024]{1,0:T(8,128)(2,1)S(1)} %fusion.12.refs_8_.refs_0_, bf16[512,1024]{1,0:T(8,128)(2,1)S(1)} %fusion.11.refs_9_.refs_1_, bf16[512,1024]{1,0:T(8,128)(2,1)S(1)} %fusion.10.refs_10_.refs_2_, bf16[512,640]{1,0:T(8,128)(2,1)} %collective-permute-done.36.refs_3_, ...), custom_call_target="tpu_custom_call" | custom-call | flops 469762048 | bytes 9568256 | tf_op jit(solution)/shard_map/pallas_call | solution.py:63
  159.0 18.9 %collective-permute-start.39 = (f32[64,1792]{1,0:T(8,128)S(1)}, f32[64,1792]{1,0:T(8,128)S(1)}, u32[]{:S(2)}, u32[]{:S(2)}) collective-permute-start(f32[64,1792]{1,0:T(8,128)S(1)} %shard_map.209), channel_id=1, source_target_pairs={{0,8},{1,9},{2,10},{3,11},{4,12},{5,13},{6,14},{7,15},{8,0},{9,1},... | collective-permute-start | bytes 1376264 | tf_op jit(solution)/shard_map/ppermute | solution.py:21
  178.1 2.1 %shard_map.210 = bf16[256,1792]{1,0:T(8,128)(2,1)S(1)} custom-call(bf16[512,1024]{1,0:T(8,128)(2,1)S(1)} %fusion.12.refs_8_.refs_0_, bf16[512,1024]{1,0:T(8,128)(2,1)S(1)} %fusion.11.refs_9_.refs_1_, bf16[512,1024]{1,0:T(8,128)(2,1)S(1)} %fusion.10.refs_10_.refs_2_, bf16[512,640]{1,0:T(8,128)(2,1)} %collective-permute-done.36.refs_3_, ...), custom_call_target="tpu_custom_call" | custom-call | flops 469762048 | bytes 9568256 | tf_op jit(solution)/shard_map/pallas_call | solution.py:63
  181.9 1.6 maximum_select_fusion
  (118 shorter events, 23.8 us)
Async XLA Ops:
  0.6 13.6 %copy-start.13 = (s32[16]{0:T(128)S(1)}, s32[16]{0:T(128)}, u32[]{:S(2)}) copy-start(s32[16]{0:T(128)} %constant.40.clone) | copy-start | bytes 196
  0.6 13.6 %copy-start.12 = (s32[16]{0:T(128)S(1)}, s32[16]{0:T(128)}, u32[]{:S(2)}) copy-start(s32[16]{0:T(128)} %constant.41.clone) | copy-start | bytes 196
  0.7 13.6 %copy-start.6 = (f32[32,3584]{1,0:T(8,128)S(1)}, f32[32,3584]{1,0:T(8,128)}, u32[]{:S(2)}) copy-start(f32[32,3584]{1,0:T(8,128)} %param.21) | copy-start | bytes 1376260
  1.6 12.8 %collective-permute-start = (bf16[256,128]{1,0:T(8,128)(2,1)S(1)}, bf16[256,128]{1,0:T(8,128)(2,1)S(1)}, u32[]{:S(2)}, u32[]{:S(2)}) collective-permute-start(bf16[256,128]{1,0:T(8,128)(2,1)S(1)} %constant_dynamic-slice_fusion.6.refs_0_), channel_id=1, source_target_pairs={{0,64},{1,65},{2,66},{3,67},{4,68},{5,69},{6,70},{7,71},{8,72},{9,... | collective-permute-start | bytes 196616 | tf_op jit(solution)/shard_map/ppermute | solution.py:21
  5.4 9.0 %collective-permute-start.1 = (bf16[256,128]{1,0:T(8,128)(2,1)S(1)}, bf16[256,128]{1,0:T(8,128)(2,1)S(1)}, u32[]{:S(2)}, u32[]{:S(2)}) collective-permute-start(bf16[256,128]{1,0:T(8,128)(2,1)S(1)} %constant_dynamic-slice_fusion.6.refs_0_), channel_id=1, source_target_pairs={{0,128},{1,129},{2,130},{3,131},{4,132},{5,133},{6,134},{7,135},{8... | collective-permute-start | bytes 196616 | tf_op jit(solution)/shard_map/ppermute | solution.py:21
  10.5 5.5 %collective-permute-start.2 = (bf16[256,128]{1,0:T(8,128)(2,1)S(1)}, bf16[256,128]{1,0:T(8,128)(2,1)S(1)}, u32[]{:S(2)}, u32[]{:S(2)}) collective-permute-start(bf16[256,128]{1,0:T(8,128)(2,1)S(1)} %constant_dynamic-slice_fusion.6.refs_0_), channel_id=1, source_target_pairs={{0,192},{1,193},{2,194},{3,195},{4,196},{5,197},{6,198},{7,199},{8... | collective-permute-start | bytes 196616 | tf_op jit(solution)/shard_map/ppermute | solution.py:21
  10.5 67.2 %collective-permute-start.26 = (bf16[256,1024]{1,0:T(8,128)(2,1)}, bf16[256,1024]{1,0:T(8,128)(2,1)}, u32[]{:S(2)}, u32[]{:S(2)}) collective-permute-start(bf16[256,1024]{1,0:T(8,128)(2,1)} %param.20), channel_id=1, source_target_pairs={{0,8},{1,9},{2,10},{3,11},{4,12},{5,13},{6,14},{7,15},{8,0},{9,1},... | collective-permute-start | bytes 1572872 | tf_op jit(solution)/shard_map/ppermute | solution.py:21
  14.3 40.6 %collective-permute-start.12 = (bf16[256,1792]{1,0:T(8,128)(2,1)}, bf16[256,1792]{1,0:T(8,128)(2,1)}, u32[]{:S(2)}, u32[]{:S(2)}) collective-permute-start(bf16[256,1792]{1,0:T(8,128)(2,1)} %get-tuple-element.80), channel_id=1, source_target_pairs={{0,8},{1,9},{2,10},{3,11},{4,12},{5,13},{6,14},{7,15},{8,0},{9,1},... | collective-permute-start | bytes 2752520 | tf_op jit(solution)/shard_map/ppermute | solution.py:21
  16.0 7.4 %collective-permute-start.3 = (bf16[1024,128]{1,0:T(8,128)(2,1)S(1)}, bf16[1024,128]{1,0:T(8,128)(2,1)S(1)}, u32[]{:S(2)}, u32[]{:S(2)}) collective-permute-start(bf16[1024,128]{1,0:T(8,128)(2,1)S(1)} %shard_map.193.refs_0_), channel_id=1, source_target_pairs={{0,16},{1,17},{2,18},{3,19},{4,20},{5,21},{6,22},{7,23},{8,24},{9,... | collective-permute-start | bytes 786440 | tf_op jit(solution)/shard_map/ppermute | solution.py:21
  17.3 12.3 %collective-permute-start.4 = (bf16[1024,128]{1,0:T(8,128)(2,1)S(1)}, bf16[1024,128]{1,0:T(8,128)(2,1)S(1)}, u32[]{:S(2)}, u32[]{:S(2)}) collective-permute-start(bf16[1024,128]{1,0:T(8,128)(2,1)S(1)} %shard_map.193.refs_0_), channel_id=1, source_target_pairs={{0,32},{1,33},{2,34},{3,35},{4,36},{5,37},{6,38},{7,39},{8,40},{9,... | collective-permute-start | bytes 786440 | tf_op jit(solution)/shard_map/ppermute | solution.py:21
  19.8 13.4 %collective-permute-start.5 = (bf16[1024,128]{1,0:T(8,128)(2,1)S(1)}, bf16[1024,128]{1,0:T(8,128)(2,1)S(1)}, u32[]{:S(2)}, u32[]{:S(2)}) collective-permute-start(bf16[1024,128]{1,0:T(8,128)(2,1)S(1)} %shard_map.193.refs_0_), channel_id=1, source_target_pairs={{0,48},{1,49},{2,50},{3,51},{4,52},{5,53},{6,54},{7,55},{8,56},{9,... | collective-permute-start | bytes 786440 | tf_op jit(solution)/shard_map/ppermute | solution.py:21
  23.4 12.1 %copy-start.7 = (f32[32,3584]{1,0:T(8,128)S(1)}, f32[32,3584]{1,0:T(8,128)}, u32[]{:S(2)}) copy-start(f32[32,3584]{1,0:T(8,128)} %param.22) | copy-start | bytes 1376260
  33.2 4.6 %collective-permute-start.6 = (bf16[4096,128]{1,0:T(8,128)(2,1)S(1)}, bf16[4096,128]{1,0:T(8,128)(2,1)S(1)}, u32[]{:S(2)}, u32[]{:S(2)}) collective-permute-start(bf16[4096,128]{1,0:T(8,128)(2,1)S(1)} %shard_map.194), channel_id=1, source_target_pairs={{0,8},{1,9},{2,10},{3,11},{4,12},{5,13},{6,14},{7,15},{8,0},{9,1},... | collective-permute-start | bytes 3145736 | tf_op jit(solution)/shard_map/ppermute | solution.py:21
  38.6 16.1 %copy-start.5 = (bf16[256,1024]{1,0:T(8,128)(2,1)S(1)}, bf16[256,1024]{1,0:T(8,128)(2,1)}, u32[]{:S(2)}) copy-start(bf16[256,1024]{1,0:T(8,128)(2,1)} %param.20) | copy-start | bytes 1572868
  39.5 3.2 %collective-permute-start.7 = (bf16[128,256]{1,0:T(8,128)(2,1)S(1)}, bf16[128,256]{1,0:T(8,128)(2,1)S(1)}, u32[]{:S(2)}, u32[]{:S(2)}) collective-permute-start(bf16[128,256]{1,0:T(8,128)(2,1)S(1)} %fusion.16.refs_0_), channel_id=1, source_target_pairs={{0,1},{1,0},{2,3},{3,2},{4,5},{5,4},{6,7},{7,6},{8,9},{9,8},{10,11... | collective-permute-start | bytes 196616 | tf_op jit(solution)/shard_map/ppermute | solution.py:21
  42.7 5.2 %collective-permute-start.10 = (bf16[256,256]{1,0:T(8,128)(2,1)S(1)}, bf16[256,256]{1,0:T(8,128)(2,1)S(1)}, u32[]{:S(2)}, u32[]{:S(2)}) collective-permute-start(bf16[256,256]{1,0:T(8,128)(2,1)S(1)} %shard_map.196.refs_0_), channel_id=1, source_target_pairs={{0,6},{1,7},{2,4},{3,5},{4,2},{5,3},{6,0},{7,1},{8,14},{9,15},{10,... | collective-permute-start | bytes 393224 | tf_op jit(solution)/shard_map/ppermute | solution.py:21
  45.5 5.7 %collective-permute-start.8 = (bf16[256,256]{1,0:T(8,128)(2,1)S(1)}, bf16[256,256]{1,0:T(8,128)(2,1)S(1)}, u32[]{:S(2)}, u32[]{:S(2)}) collective-permute-start(bf16[256,256]{1,0:T(8,128)(2,1)S(1)} %shard_map.196.refs_0_), channel_id=1, source_target_pairs={{0,2},{1,3},{2,0},{3,1},{4,6},{5,7},{6,4},{7,5},{8,10},{9,11},{10,... | collective-permute-start | bytes 393224 | tf_op jit(solution)/shard_map/ppermute | solution.py:21
  45.5 6.4 %collective-permute-start.9 = (bf16[256,256]{1,0:T(8,128)(2,1)S(1)}, bf16[256,256]{1,0:T(8,128)(2,1)S(1)}, u32[]{:S(2)}, u32[]{:S(2)}) collective-permute-start(bf16[256,256]{1,0:T(8,128)(2,1)S(1)} %shard_map.196.refs_0_), channel_id=1, source_target_pairs={{0,4},{1,5},{2,6},{3,7},{4,0},{5,1},{6,2},{7,3},{8,12},{9,13},{10,... | collective-permute-start | bytes 393224 | tf_op jit(solution)/shard_map/ppermute | solution.py:21
  47.9 15.0 %collective-permute-start.25 = (f32[64,1792]{1,0:T(8,128)S(1)}, f32[64,1792]{1,0:T(8,128)}, u32[]{:S(2)}, u32[]{:S(2)}) collective-permute-start(f32[64,1792]{1,0:T(8,128)S(1)} %constant_dynamic-slice_fusion.3), channel_id=1, source_target_pairs={{0,8},{1,9},{2,10},{3,11},{4,12},{5,13},{6,14},{7,15},{8,0},{9,1},... | collective-permute-start | bytes 1376264 | tf_op jit(solution)/shard_map/ppermute | solution.py:21
  51.9 4.2 %collective-permute-start.11 = (bf16[1024,256]{1,0:T(8,128)(2,1)S(1)}, bf16[1024,256]{1,0:T(8,128)(2,1)S(1)}, u32[]{:S(2)}, u32[]{:S(2)}) collective-permute-start(bf16[1024,256]{1,0:T(8,128)(2,1)S(1)} %shard_map.197.refs_1_), channel_id=1, source_target_pairs={{0,8},{1,9},{2,10},{3,11},{4,12},{5,13},{6,14},{7,15},{8,0},{9,1},... | collective-permute-start | bytes 1572872 | tf_op jit(solution)/shard_map/ppermute | solution.py:21
  58.0 16.7 %collective-permute-start.13 = (bf16[512,640]{1,0:T(8,128)(2,1)S(1)}, bf16[512,640]{1,0:T(8,128)(2,1)S(1)}, u32[]{:S(2)}, u32[]{:S(2)}) collective-permute-start(bf16[512,640]{1,0:T(8,128)(2,1)S(1)} %get-tuple-element.44), channel_id=1, source_target_pairs={{0,16},{1,17},{2,18},{3,19},{4,20},{5,21},{6,22},{7,23},{8,24},{9,... | collective-permute-start | bytes 1966088 | tf_op jit(solution)/shard_map/ppermute | solution.py:21
  58.3 17.4 %collective-permute-start.14 = (bf16[512,640]{1,0:T(8,128)(2,1)S(1)}, bf16[512,640]{1,0:T(8,128)(2,1)S(1)}, u32[]{:S(2)}, u32[]{:S(2)}) collective-permute-start(bf16[512,640]{1,0:T(8,128)(2,1)S(1)} %get-tuple-element.45), channel_id=1, source_target_pairs={{0,48},{1,49},{2,50},{3,51},{4,52},{5,53},{6,54},{7,55},{8,56},{9,... | collective-permute-start | bytes 1966088 | tf_op jit(solution)/shard_map/ppermute | solution.py:21
  58.6 16.1 %collective-permute-start.15 = (bf16[512,512]{1,0:T(8,128)(2,1)S(1)}, bf16[512,512]{1,0:T(8,128)(2,1)S(1)}, u32[]{:S(2)}, u32[]{:S(2)}) collective-permute-start(bf16[512,512]{1,0:T(8,128)(2,1)S(1)} %get-tuple-element.46), channel_id=1, source_target_pairs={{0,64},{1,65},{2,66},{3,67},{4,68},{5,69},{6,70},{7,71},{8,200},{9... | collective-permute-start | bytes 1572872 | tf_op jit(solution)/shard_map/ppermute | solution.py:21
  76.0 12.1 %collective-permute-start.16 = (bf16[256,640]{1,0:T(8,128)(2,1)S(1)}, bf16[256,640]{1,0:T(8,128)(2,1)S(1)}, u32[]{:S(2)}, u32[]{:S(2)}) collective-permute-start(bf16[256,640]{1,0:T(8,128)(2,1)S(1)} %get-tuple-element.50), channel_id=1, source_target_pairs={{0,48},{1,49},{2,50},{3,51},{4,52},{5,53},{6,54},{7,55},{8,56},{9,... | collective-permute-start | bytes 983048 | tf_op jit(solution)/shard_map/ppermute | solution.py:21
  77.5 10.6 %collective-permute-start.17 = (bf16[256,640]{1,0:T(8,128)(2,1)S(1)}, bf16[256,640]{1,0:T(8,128)(2,1)S(1)}, u32[]{:S(2)}, u32[]{:S(2)}) collective-permute-start(bf16[256,640]{1,0:T(8,128)(2,1)S(1)} %get-tuple-element.51), channel_id=1, source_target_pairs={{0,16},{1,17},{2,18},{3,19},{4,20},{5,21},{6,22},{7,23},{8,24},{9,... | collective-permute-start | bytes 983048 | tf_op jit(solution)/shard_map/ppermute | solution.py:21
  78.8 9.4 %collective-permute-start.18 = (bf16[256,512]{1,0:T(8,128)(2,1)S(1)}, bf16[256,512]{1,0:T(8,128)(2,1)S(1)}, u32[]{:S(2)}, u32[]{:S(2)}) collective-permute-start(bf16[256,512]{1,0:T(8,128)(2,1)S(1)} %get-tuple-element.52), channel_id=1, source_target_pairs={{0,192},{1,193},{2,194},{3,195},{4,196},{5,197},{6,198},{7,199},{8... | collective-permute-start | bytes 786440 | tf_op jit(solution)/shard_map/ppermute | solution.py:21
  88.3 10.5 %collective-permute-start.19 = (bf16[128,640]{1,0:T(8,128)(2,1)S(1)}, bf16[128,640]{1,0:T(8,128)(2,1)S(1)}, u32[]{:S(2)}, u32[]{:S(2)}) collective-permute-start(bf16[128,640]{1,0:T(8,128)(2,1)S(1)} %get-tuple-element.56), channel_id=1, source_target_pairs={{0,64},{1,65},{2,66},{3,67},{4,68},{5,69},{6,70},{7,71},{8,72},{9,... | collective-permute-start | bytes 491528 | tf_op jit(solution)/shard_map/ppermute | solution.py:21
  89.2 9.6 %collective-permute-start.20 = (bf16[128,640]{1,0:T(8,128)(2,1)S(1)}, bf16[128,640]{1,0:T(8,128)(2,1)S(1)}, u32[]{:S(2)}, u32[]{:S(2)}) collective-permute-start(bf16[128,640]{1,0:T(8,128)(2,1)S(1)} %get-tuple-element.57), channel_id=1, source_target_pairs={{0,192},{1,193},{2,194},{3,195},{4,196},{5,197},{6,198},{7,199},{8... | collective-permute-start | bytes 491528 | tf_op jit(solution)/shard_map/ppermute | solution.py:21
  93.5 5.3 %collective-permute-start.21 = (bf16[128,512]{1,0:T(8,128)(2,1)S(1)}, bf16[128,512]{1,0:T(8,128)(2,1)S(1)}, u32[]{:S(2)}, u32[]{:S(2)}) collective-permute-start(bf16[128,512]{1,0:T(8,128)(2,1)S(1)} %get-tuple-element.58), channel_id=1, source_target_pairs={{0,16},{1,17},{2,18},{3,19},{4,20},{5,21},{6,22},{7,23},{8,56},{9,... | collective-permute-start | bytes 393224 | tf_op jit(solution)/shard_map/ppermute | solution.py:21
  98.9 6.6 %collective-permute-start.22 = (bf16[64,640]{1,0:T(8,128)(2,1)S(1)}, bf16[64,640]{1,0:T(8,128)(2,1)S(1)}, u32[]{:S(2)}, u32[]{:S(2)}) collective-permute-start(bf16[64,640]{1,0:T(8,128)(2,1)S(1)} %get-tuple-element.62), channel_id=1, source_target_pairs={{0,192},{1,193},{2,194},{3,195},{4,196},{5,197},{6,198},{7,199},{8... | collective-permute-start | bytes 245768 | tf_op jit(solution)/shard_map/ppermute | solution.py:21
  102.4 4.8 %collective-permute-start.23 = (bf16[64,640]{1,0:T(8,128)(2,1)S(1)}, bf16[64,640]{1,0:T(8,128)(2,1)S(1)}, u32[]{:S(2)}, u32[]{:S(2)}) collective-permute-start(bf16[64,640]{1,0:T(8,128)(2,1)S(1)} %get-tuple-element.63), channel_id=1, source_target_pairs={{0,64},{1,65},{2,66},{3,67},{4,68},{5,69},{6,70},{7,71},{8,72},{9,... | collective-permute-start | bytes 245768 | tf_op jit(solution)/shard_map/ppermute | solution.py:21
  102.5 3.1 %collective-permute-start.24 = (bf16[64,512]{1,0:T(8,128)(2,1)S(1)}, bf16[64,512]{1,0:T(8,128)(2,1)S(1)}, u32[]{:S(2)}, u32[]{:S(2)}) collective-permute-start(bf16[64,512]{1,0:T(8,128)(2,1)S(1)} %get-tuple-element.64), channel_id=1, source_target_pairs={{0,48},{1,49},{2,50},{3,51},{4,52},{5,53},{6,54},{7,55},{8,24},{9,... | collective-permute-start | bytes 196616 | tf_op jit(solution)/shard_map/ppermute | solution.py:21
  109.2 6.3 %collective-permute-start.27 = (bf16[64,640]{1,0:T(8,128)(2,1)S(1)}, bf16[64,640]{1,0:T(8,128)(2,1)S(1)}, u32[]{:S(2)}, u32[]{:S(2)}) collective-permute-start(bf16[64,640]{1,0:T(8,128)(2,1)S(1)} %get-tuple-element.67.refs_0_), channel_id=1, source_target_pairs={{0,192},{1,193},{2,194},{3,195},{4,196},{5,197},{6,198},{7,199},{8... | collective-permute-start | bytes 245768 | tf_op jit(solution)/shard_map/ppermute | solution.py:21
  110.4 5.1 %collective-permute-start.28 = (bf16[64,640]{1,0:T(8,128)(2,1)S(1)}, bf16[64,640]{1,0:T(8,128)(2,1)S(1)}, u32[]{:S(2)}, u32[]{:S(2)}) collective-permute-start(bf16[64,640]{1,0:T(8,128)(2,1)S(1)} %get-tuple-element.68.refs_2_), channel_id=1, source_target_pairs={{0,64},{1,65},{2,66},{3,67},{4,68},{5,69},{6,70},{7,71},{8,72},{9,... | collective-permute-start | bytes 245768 | tf_op jit(solution)/shard_map/ppermute | solution.py:21
  110.4 3.1 %collective-permute-start.29 = (bf16[64,512]{1,0:T(8,128)(2,1)S(1)}, bf16[64,512]{1,0:T(8,128)(2,1)S(1)}, u32[]{:S(2)}, u32[]{:S(2)}) collective-permute-start(bf16[64,512]{1,0:T(8,128)(2,1)S(1)} %get-tuple-element.69.refs_4_), channel_id=1, source_target_pairs={{0,48},{1,49},{2,50},{3,51},{4,52},{5,53},{6,54},{7,55},{8,24},{9,... | collective-permute-start | bytes 196616 | tf_op jit(solution)/shard_map/ppermute | solution.py:21
  115.5 8.2 %collective-permute-start.30 = (bf16[128,640]{1,0:T(8,128)(2,1)S(1)}, bf16[128,640]{1,0:T(8,128)(2,1)S(1)}, u32[]{:S(2)}, u32[]{:S(2)}) collective-permute-start(bf16[128,640]{1,0:T(8,128)(2,1)S(1)} %get-tuple-element.70.refs_0_), channel_id=1, source_target_pairs={{0,64},{1,65},{2,66},{3,67},{4,68},{5,69},{6,70},{7,71},{8,72},{9,... | collective-permute-start | bytes 491528 | tf_op jit(solution)/shard_map/ppermute | solution.py:21
  116.3 7.9 %collective-permute-start.31 = (bf16[128,640]{1,0:T(8,128)(2,1)S(1)}, bf16[128,640]{1,0:T(8,128)(2,1)S(1)}, u32[]{:S(2)}, u32[]{:S(2)}) collective-permute-start(bf16[128,640]{1,0:T(8,128)(2,1)S(1)} %get-tuple-element.71.refs_2_), channel_id=1, source_target_pairs={{0,192},{1,193},{2,194},{3,195},{4,196},{5,197},{6,198},{7,199},{8... | collective-permute-start | bytes 491528 | tf_op jit(solution)/shard_map/ppermute | solution.py:21
  118.6 5.0 %collective-permute-start.32 = (bf16[128,512]{1,0:T(8,128)(2,1)S(1)}, bf16[128,512]{1,0:T(8,128)(2,1)S(1)}, u32[]{:S(2)}, u32[]{:S(2)}) collective-permute-start(bf16[128,512]{1,0:T(8,128)(2,1)S(1)} %get-tuple-element.72.refs_4_), channel_id=1, source_target_pairs={{0,16},{1,17},{2,18},{3,19},{4,20},{5,21},{6,22},{7,23},{8,56},{9,... | collective-permute-start | bytes 393224 | tf_op jit(solution)/shard_map/ppermute | solution.py:21
  124.2 12.3 %collective-permute-start.33 = (bf16[256,640]{1,0:T(8,128)(2,1)S(1)}, bf16[256,640]{1,0:T(8,128)(2,1)S(1)}, u32[]{:S(2)}, u32[]{:S(2)}) collective-permute-start(bf16[256,640]{1,0:T(8,128)(2,1)S(1)} %get-tuple-element.73.refs_0_), channel_id=1, source_target_pairs={{0,48},{1,49},{2,50},{3,51},{4,52},{5,53},{6,54},{7,55},{8,56},{9,... | collective-permute-start | bytes 983048 | tf_op jit(solution)/shard_map/ppermute | solution.py:21
  125.7 10.9 %collective-permute-start.34 = (bf16[256,640]{1,0:T(8,128)(2,1)S(1)}, bf16[256,640]{1,0:T(8,128)(2,1)S(1)}, u32[]{:S(2)}, u32[]{:S(2)}) collective-permute-start(bf16[256,640]{1,0:T(8,128)(2,1)S(1)} %get-tuple-element.74.refs_2_), channel_id=1, source_target_pairs={{0,16},{1,17},{2,18},{3,19},{4,20},{5,21},{6,22},{7,23},{8,24},{9,... | collective-permute-start | bytes 983048 | tf_op jit(solution)/shard_map/ppermute | solution.py:21
  125.7 10.8 %collective-permute-start.35 = (bf16[256,512]{1,0:T(8,128)(2,1)S(1)}, bf16[256,512]{1,0:T(8,128)(2,1)S(1)}, u32[]{:S(2)}, u32[]{:S(2)}) collective-permute-start(bf16[256,512]{1,0:T(8,128)(2,1)S(1)} %get-tuple-element.75.refs_4_), channel_id=1, source_target_pairs={{0,192},{1,193},{2,194},{3,195},{4,196},{5,197},{6,198},{7,199},{8... | collective-permute-start | bytes 786440 | tf_op jit(solution)/shard_map/ppermute | solution.py:21
  137.9 18.9 %collective-permute-start.36 = (bf16[512,640]{1,0:T(8,128)(2,1)}, bf16[512,640]{1,0:T(8,128)(2,1)}, u32[]{:S(2)}, u32[]{:S(2)}) collective-permute-start(bf16[512,640]{1,0:T(8,128)(2,1)} %get-tuple-element.76.refs_3_), channel_id=1, source_target_pairs={{0,16},{1,17},{2,18},{3,19},{4,20},{5,21},{6,22},{7,23},{8,24},{9,... | collective-permute-start | bytes 1966088 | tf_op jit(solution)/shard_map/ppermute | solution.py:21
  138.2 18.6 %collective-permute-start.37 = (bf16[512,640]{1,0:T(8,128)(2,1)}, bf16[512,640]{1,0:T(8,128)(2,1)}, u32[]{:S(2)}, u32[]{:S(2)}) collective-permute-start(bf16[512,640]{1,0:T(8,128)(2,1)} %get-tuple-element.77.refs_4_), channel_id=1, source_target_pairs={{0,48},{1,49},{2,50},{3,51},{4,52},{5,53},{6,54},{7,55},{8,56},{9,... | collective-permute-start | bytes 1966088 | tf_op jit(solution)/shard_map/ppermute | solution.py:21
  139.7 17.1 %collective-permute-start.38 = (bf16[512,512]{1,0:T(8,128)(2,1)}, bf16[512,512]{1,0:T(8,128)(2,1)}, u32[]{:S(2)}, u32[]{:S(2)}) collective-permute-start(bf16[512,512]{1,0:T(8,128)(2,1)} %get-tuple-element.78.refs_5_), channel_id=1, source_target_pairs={{0,64},{1,65},{2,66},{3,67},{4,68},{5,69},{6,70},{7,71},{8,200},{9... | collective-permute-start | bytes 1572872 | tf_op jit(solution)/shard_map/ppermute | solution.py:21
  143.1 15.8 %copy-start.2 = (f32[64,1792]{1,0:T(8,128)S(1)}, f32[64,1792]{1,0:T(8,128)}, u32[]{:S(2)}) copy-start(f32[64,1792]{1,0:T(8,128)} %copy-done.1) | copy-start | bytes 1376260
  143.1 15.8 %copy-start.4 = (f32[64,1792]{1,0:T(8,128)S(1)}, f32[64,1792]{1,0:T(8,128)}, u32[]{:S(2)}) copy-start(f32[64,1792]{1,0:T(8,128)} %copy-done.3) | copy-start | bytes 1376260
  159.0 21.2 %collective-permute-start.39 = (f32[64,1792]{1,0:T(8,128)S(1)}, f32[64,1792]{1,0:T(8,128)S(1)}, u32[]{:S(2)}, u32[]{:S(2)}) collective-permute-start(f32[64,1792]{1,0:T(8,128)S(1)} %shard_map.209), channel_id=1, source_target_pairs={{0,8},{1,9},{2,10},{3,11},{4,12},{5,13},{6,14},{7,15},{8,0},{9,1},... | collective-permute-start | bytes 1376264 | tf_op jit(solution)/shard_map/ppermute | solution.py:21
  178.0 3.9 %collective-permute-start.40 = (bf16[256,1792]{1,0:T(8,128)(2,1)S(1)}, bf16[256,1792]{1,0:T(8,128)(2,1)S(1)}, u32[]{:S(2)}, u32[]{:S(2)}) collective-permute-start(bf16[256,1792]{1,0:T(8,128)(2,1)S(1)} %shard_map.208.refs_3_), channel_id=1, source_target_pairs={{0,8},{1,9},{2,10},{3,11},{4,12},{5,13},{6,14},{7,15},{8,0},{9,1},... | collective-permute-start | bytes 2752520 | tf_op jit(solution)/shard_map/ppermute | solution.py:21
  (8 other events, 24.0 us)
